TPU v7x, 512 devices: a whole 4x4x16 slice. The times are simulated.
512 devices in a mesh: ctx: 16 (over z), exp: 32 (over y, x, core).
Axes of the slice: x: 4, y: 4, z: 16, core: 2. Of those that a mesh axis runs over, the one named last changes fastest.
Arguments:
- queries: bfloat16 [1024, 4096], P('ctx', 'exp'), may hold values from -36 to 36
- keys: bfloat16 [1024, 1024], P('ctx'), may hold values from -4 to 4
- values: bfloat16 [1024, 1024], P('ctx'), may hold values from -6 to 6
- out_proj: bfloat16 [4096, 4096], P('ctx', 'exp'), may hold values from -0.09375 to 0.09375
- residual_in: bfloat16 [1024, 4096], P('ctx', 'exp'), may hold values from -48 to 48
- norm_gain: float32 [4096], P('exp'), may hold values from 0.1 to 1.9
- routes: int32 [1024, 2], replicated, may hold values from 0 to 7, all different within a row; in each aligned block of 64 rows (0 to 63, 64 to 127, ...) at most 16 rows name the same one
- gate_wts: float32 [1024, 2], P('ctx'), may hold values from 0.2 to 1
- w_gate: bfloat16 [4096, 65536], P(None, ('exp', 'ctx')), may hold values from -0.09375 to 0.09375
- w_up: bfloat16 [4096, 65536], P(None, ('exp', 'ctx')), may hold values from -0.09375 to 0.09375
- w_down: bfloat16 [65536, 4096], P(('exp', 'ctx')), may hold values from -0.25 to 0.25
Outputs:
- residual_out: bfloat16 [1024, 4096], P('ctx', 'exp')
- expert_out: bfloat16 [1024, 4096], P('ctx', 'exp')
Inputs may be any that keep to these rules, and one draw needn't show every extreme that they name: `routes`: within the 64 tokens of one ctx shard no expert is named more than 16 times, and in every draw some expert is named exactly 16 times within some shard; the two experts of a token differ.
All inputs are finite; a program needn't handle non-finite values.
Results may differ from a plain program's by a relative error of at most 0.033.
Values may be sent and summed in bfloat16 or wider, within the bound.
No kernel may reach another device: no remote copies, remote signals or barrier semaphores. Data moves between devices by JAX's collectives and lax.ppermute only.
A program may use at most 64 MiB of HBM per device.

v0:
```python
import math

import jax
import jax.numpy as jnp
import numpy as np
from jax import lax
from jax.sharding import PartitionSpec as P

D = 4096
QUERY_HEAD_COUNT = 32
KEY_VALUE_HEADS = 8
HEAD_SIZE = 128
EXPERTS = 8
TOP = 2
CAP = 16


def slot_table(routes, shard_count, seg_len):
    flat_routes = routes.reshape(shard_count, seg_len * TOP)
    one_hot = (
        flat_routes[:, :, None] == jnp.arange(EXPERTS, dtype=jnp.int32)[None, None, :]
    ).astype(jnp.int32)
    earlier = jnp.cumsum(one_hot, axis=1) - one_hot
    return (jnp.sum(earlier * one_hot, axis=2), jnp.sum(one_hot, axis=1))


def expert_rows(rows_in, w_gate, w_up, w_down):
    gate_val = jnp.dot(rows_in, w_gate, preferred_element_type=jnp.float32)
    up_val = jnp.dot(rows_in, w_up, preferred_element_type=jnp.float32)
    hidden = (jax.nn.silu(gate_val) * up_val).astype(jnp.bfloat16)
    return jnp.dot(hidden, w_down, preferred_element_type=jnp.float32)


def per_device(
    queries, keys, values, out_proj, residual_in, norm_gain, routes, gate_wts, w_gate, w_up, w_down
):
    ctx_count = lax.axis_size("ctx")
    exp_count = lax.axis_size("exp")
    ctx_rank = lax.axis_index("ctx")
    exp_rank = lax.axis_index("exp")
    seg_len = queries.shape[0]
    heads_dev = queries.shape[1] // HEAD_SIZE
    query_group_width = QUERY_HEAD_COUNT // KEY_VALUE_HEADS
    kv_dev = max(1, heads_dev // query_group_width)
    kv_first = exp_rank * heads_dev // query_group_width
    key_part = lax.dynamic_slice_in_dim(keys, kv_first * HEAD_SIZE, kv_dev * HEAD_SIZE, 1)
    value_part = lax.dynamic_slice_in_dim(values, kv_first * HEAD_SIZE, kv_dev * HEAD_SIZE, 1)
    head_map = np.zeros(heads_dev, dtype=np.int32)
    query_pos = ctx_rank * seg_len + jnp.arange(seg_len, dtype=jnp.int32)
    query_heads = queries.reshape(seg_len, heads_dev, HEAD_SIZE)
    score_scale = 1.0 / math.sqrt(HEAD_SIZE)
    run_max = jnp.full((heads_dev, seg_len), -1e30, jnp.float32)
    run_sum = jnp.zeros((heads_dev, seg_len), jnp.float32)
    run_acc = jnp.zeros((heads_dev, seg_len, HEAD_SIZE), jnp.float32)
    key_piece = lax.all_gather(key_part, "ctx", axis=0, tiled=True)
    value_piece = lax.all_gather(value_part, "ctx", axis=0, tiled=True)
    piece_rows = key_piece.shape[0]
    key_heads = key_piece.reshape(piece_rows, kv_dev, HEAD_SIZE)[:, head_map, :]
    value_heads = value_piece.reshape(piece_rows, kv_dev, HEAD_SIZE)[:, head_map, :]
    scores = (
        jnp.einsum("shd,nhd->hsn", query_heads, key_heads, preferred_element_type=jnp.float32)
        * score_scale
    )
    key_pos = jnp.arange(piece_rows, dtype=jnp.int32)
    visible = (query_pos[:, None] >= key_pos[None, :])[None, :, :]
    scores = jnp.where(visible, scores, -1e30)
    new_max = jnp.maximum(run_max, jnp.max(scores, axis=2))
    weights = jnp.where(visible, jnp.exp(scores - new_max[:, :, None]), 0.0)
    factor = jnp.exp(run_max - new_max)
    new_sum = run_sum * factor + jnp.sum(weights, axis=2)
    added = jnp.einsum(
        "hsn,nhd->hsd",
        weights.astype(jnp.bfloat16),
        value_heads,
        preferred_element_type=jnp.float32,
    )
    run_max, run_sum, run_acc = (new_max, new_sum, run_acc * factor[:, :, None] + added)
    attn_local = (
        (run_acc / run_sum[:, :, None])
        .transpose(1, 0, 2)
        .reshape(seg_len, heads_dev * HEAD_SIZE)
        .astype(jnp.bfloat16)
    )
    attn_all = lax.all_gather(attn_local, "exp", axis=1, tiled=True)
    projected = jnp.dot(
        attn_all,
        lax.all_gather(out_proj, "ctx", axis=0, tiled=True),
        preferred_element_type=jnp.float32,
    )
    residual = residual_in.astype(jnp.float32) + projected
    residual_out = residual.astype(jnp.bfloat16)
    sq_mean = lax.psum(jnp.sum(residual * residual, axis=1), "exp") / D
    normed = (residual * lax.rsqrt(sq_mean + 1e-05)[:, None] * norm_gain[None, :]).astype(
        jnp.bfloat16
    )
    quarters = exp_count // EXPERTS
    my_expert = exp_rank // quarters
    slot_all, counts_all = slot_table(routes, ctx_count, seg_len)
    own_slot = lax.dynamic_index_in_dim(slot_all, ctx_rank, 0, keepdims=False).reshape(seg_len, TOP)
    own_route = lax.dynamic_slice_in_dim(routes, ctx_rank * seg_len, seg_len, 0)
    slot_ids = jnp.arange(CAP, dtype=jnp.int32)
    full_rows = lax.all_gather(normed, "exp", axis=1, tiled=True)
    chosen = (
        ((own_route[None, :, :] == my_expert) & (own_slot[None, :, :] == slot_ids[:, None, None]))
        .astype(jnp.int32)
        .sum(axis=2)
        .astype(jnp.bfloat16)
    )
    picked = jnp.dot(chosen, full_rows, preferred_element_type=jnp.float32).astype(jnp.bfloat16)
    rows_all = lax.all_gather(picked, "ctx", axis=0, tiled=True)
    summed = lax.psum_scatter(
        expert_rows(rows_all, w_gate, w_up, w_down).astype(jnp.bfloat16),
        "ctx",
        scatter_dimension=0,
        tiled=True,
    )
    returned = lax.all_to_all(
        summed.reshape(1, CAP, summed.shape[1]), "exp", split_axis=2, concat_axis=0, tiled=True
    )
    owner_expert = jnp.arange(exp_count, dtype=jnp.int32) // quarters
    match_expert = (own_route[:, :, None] == owner_expert[None, None, :]).astype(jnp.float32)
    match_slot = (own_slot[:, :, None] == slot_ids[None, None, :]).astype(jnp.float32)
    combine = jnp.einsum(
        "tk,tkj,tks->tjs", gate_wts, match_expert, match_slot, precision=lax.Precision.HIGHEST
    ).reshape(seg_len, exp_count * CAP)
    flat_returned = returned.reshape(exp_count * CAP, returned.shape[2]).astype(jnp.float32)
    expert_out = jnp.dot(combine, flat_returned, precision=lax.Precision.HIGHEST).astype(
        jnp.bfloat16
    )
    return (residual_out, expert_out)


def solution(mesh):
    placed = (
        P("ctx", "exp"),
        P("ctx", None),
        P("ctx", None),
        P("ctx", "exp"),
        P("ctx", "exp"),
        P("exp"),
        P(),
        P("ctx", None),
        P(None, ("exp", "ctx")),
        P(None, ("exp", "ctx")),
        P(("exp", "ctx"), None),
    )
    return jax.shard_map(
        per_device,
        mesh=mesh,
        in_specs=placed,
        out_specs=(P("ctx", "exp"), P("ctx", "exp")),
        check_vma=False,
    )
```

profile of v0, /device:TPU:1, one launch (start us, length us, event | category | flops | bytes accessed | tf_op | source)
XLA Modules:
  0.0 401.2 jit_solution(1183322907352983559)
XLA Ops:
  7.2 0.0 copy-start
  7.2 0.0 copy-start.3
  7.2 0.0 all-gather.3.cloned.1.call-start
  7.2 0.7 all-gather.3.cloned.1.call-update
  7.9 0.0 all-gather.5.cloned.1.call-start
  8.0 0.0 copy-start.2
  8.0 0.9 copy.43
  8.9 0.3 eq.66
  9.2 0.1 copy.44
  9.3 2.8 select_reduce_fusion
  12.1 0.2 dynamic-slice_reduce_fusion
  12.3 0.1 eq.70
  12.4 0.1 copy.47
  12.5 0.8 broadcast_compare_fusion
  13.3 0.7 constant_dynamic-slice_fusion.2
  14.0 0.7 constant_dynamic-slice_fusion.1
  14.7 0.0 copy-start.5
  14.7 31.5 %all_gather.18 = bf16[1024,128]{1,0:T(8,128)(2,1)S(1)} all-gather(bf16[64,128]{1,0:T(8,128)(2,1)S(1)} %constant_dynamic-slice_fusion.2), channel_id=1, replica_groups=mesh['ctx'=16,'exp'=32] {'ctx'}, dimensions={0}, use_global_device_ids=true | all-gather | bytes 278528 | tf_op jit(solution)/shard_map/all_gather | solution.py:55
  46.3 21.8 %all_gather.19 = bf16[1024,128]{1,0:T(8,128)(2,1)S(1)} all-gather(bf16[64,128]{1,0:T(8,128)(2,1)S(1)} %constant_dynamic-slice_fusion.1), channel_id=1, replica_groups=mesh['ctx'=16,'exp'=32] {'ctx'}, dimensions={0}, use_global_device_ids=true | all-gather | bytes 278528 | tf_op jit(solution)/shard_map/all_gather | solution.py:56
  68.1 0.0 copy-done.3
  68.1 0.3 fusion.36
  68.4 0.2 fusion.10
  68.6 0.3 fusion.8
  68.9 37.8 %all_gather.20 = bf16[64,4096]{1,0:T(8,128)(2,1)S(1)} all-gather(bf16[64,128]{1,0:T(8,128)(2,1)S(1)} %fusion.8), channel_id=1, replica_groups=mesh['ctx'=16,'exp'=32] {'exp'}, dimensions={1}, use_global_device_ids=true | all-gather | bytes 540672 | tf_op jit(solution)/shard_map/all_gather | solution.py:84
  106.7 0.0 all-gather.3.cloned.1.call-done
  106.7 0.0 copy-done.2
  106.7 1.6 multiply_reduce_fusion
  108.3 62.2 %psum.7 = f32[64]{0:T(128)S(1)} all-reduce(f32[64]{0:T(128)S(1)} %get-tuple-element.10), channel_id=1, replica_groups=mesh['ctx'=16,'exp'=32] {'exp'}, use_global_device_ids=true, to_apply=%region_6.7 | all-reduce | flops 64 | bytes 512 | tf_op jit(solution)/shard_map/psum | solution.py:92
  170.5 0.0 copy-done.5
  170.5 0.6 multiply_convert_fusion
  171.1 25.0 %all_gather.22 = bf16[64,4096]{1,0:T(8,128)(2,1)S(1)} all-gather(bf16[64,128]{1,0:T(8,128)(2,1)S(1)} %get-tuple-element.4), channel_id=1, replica_groups=mesh['ctx'=16,'exp'=32] {'exp'}, dimensions={1}, use_global_device_ids=true | all-gather | bytes 540672 | tf_op jit(solution)/shard_map/all_gather | solution.py:102
  196.1 0.8 convolution_convert_fusion.1
  197.0 0.0 all-gather.5.cloned.1.call-update
  197.0 0.2 reduce-scatter.2.cloned.1.call-start
  197.2 59.8 %all-gather.5.cloned.1.call-done = bf16[256,4096]{1,0:T(8,128)(2,1)} async-done(((bf16[16,4096]{1,0:T(8,128)(2,1)}), bf16[256,4096]{1,0:T(8,128)(2,1)}) %all-gather.5.cloned.1.call-update) | async-done | bytes 2097168 | tf_op jit(solution)/shard_map/all_gather | solution.py:110
  257.0 0.0 copy-start.1
  257.0 2.7 fusion.37
  259.7 0.0 copy-done
  259.7 0.0 copy-done.1
  259.7 3.9 convolution_convert_fusion
  263.6 0.0 copy-start.4
  263.6 0.0 reduce-scatter.2.cloned.1.call-update
  263.7 0.1 copy.42
  263.8 0.6 copy-done.4
  264.3 0.1 copy.45
  264.4 68.4 %reduce-scatter.2.cloned.1.call-done = bf16[16,4096]{1,0:T(8,128)(2,1)} async-done(((bf16[256,4096]{1,0:T(8,128)(2,1)}), bf16[16,4096]{1,0:T(8,128)(2,1)}) %reduce-scatter.2.cloned.1.call-update) | async-done | bytes 131088 | tf_op jit(solution)/shard_map/reduce_scatter | solution.py:111
  332.9 4.3 %copy.48 = bf16[1,16,4096]{1,0,2:T(2,128)(2,1)S(1)} copy(bf16[1,16,4096]{2,1,0:T(8,128)(2,1)} %bitcast.36) | data formatting | bytes 262144 | tf_op jit(solution)/shard_map/reshape | solution.py:118
  337.2 0.5 broadcast.104
  337.7 23.4 %reduce.6 = bf16[4096,16]{1,0:T(8,128)(2,1)} reduce(bf16[4096,1,16]{2,1,0:T(2,128)(2,1)S(1)} %bitcast.30, bf16[]{:T(256)} %broadcast.104), dimensions={1}, to_apply=%bitcast.14.reduce_sub_computation | reduce | bytes 262146
  361.1 3.1 reshape.120
  364.2 17.9 %all-to-all-start = ((bf16[32,2,1024]{2,1,0:T(2,128)(2,1)}), bf16[32,2,1024]{2,1,0:T(2,128)(2,1)S(1)}, u32[]{:S(2)}, u32[]{:S(2)}) async-start(bf16[32,2,1024]{2,1,0:T(2,128)(2,1)} %reshape.120), calls=%async_computation.1 | async-start | bytes 262144 | tf_op jit(solution)/shard_map/all_to_all | solution.py:117
  382.1 0.9 fusion.21
  383.0 0.3 copy.46
  383.3 6.5 %all-to-all-done = bf16[32,2,1024]{2,1,0:T(2,128)(2,1)S(1)} async-done(((bf16[32,2,1024]{2,1,0:T(2,128)(2,1)}), bf16[32,2,1024]{2,1,0:T(2,128)(2,1)S(1)}, u32[]{:S(2)}, u32[]{:S(2)}) %all-to-all-start) | async-done | bytes 131104 | tf_op jit(solution)/shard_map/all_to_all | solution.py:117
  389.7 1.8 reshape.121
  391.6 2.0 copy.49
  393.6 0.1 copy.50
  393.7 1.0 convolution_convert_fusion.2
  (8 shorter events, 0.1 us)
Async XLA Ops:
  7.2 252.6 %copy-start = (bf16[128,4096]{1,0:T(8,128)(2,1)S(1)}, bf16[128,4096]{1,0:T(8,128)(2,1)}, u32[]{:S(2)}) copy-start(bf16[128,4096]{1,0:T(8,128)(2,1)} %param.24) | copy-start | bytes 3145732
  7.2 60.9 %copy-start.3 = (bf16[64,128]{1,0:T(8,128)(2,1)S(1)}, bf16[64,128]{1,0:T(8,128)(2,1)}, u32[]{:S(2)}) copy-start(bf16[64,128]{1,0:T(8,128)(2,1)} %param.14) | copy-start | bytes 49156
  7.2 99.5 %all-gather.3.cloned.1.call-start = ((), (), s32[]{:S(2)}) async-start(), calls=%async_computation.2 | async-start | bytes 1114112 | tf_op jit(solution)/shard_map/all_gather | solution.py:87
  7.9 249.1 %all-gather.5.cloned.1.call-start = ((), (), s32[]{:S(2)}) async-start(), calls=%async_computation.3 | async-start | bytes 2228224 | tf_op jit(solution)/shard_map/all_gather | solution.py:110
  8.0 98.7 %copy-start.2 = (bf16[64,128]{1,0:T(8,128)(2,1)S(1)}, bf16[64,128]{1,0:T(8,128)(2,1)}, u32[]{:S(2)}) copy-start(bf16[64,128]{1,0:T(8,128)(2,1)} %param.18) | copy-start | bytes 49156
  14.7 155.8 %copy-start.5 = (f32[128]{0:T(128)S(1)}, f32[128]{0:T(128)}, u32[]{:S(2)}) copy-start(f32[128]{0:T(128)} %param.19) | copy-start | bytes 1540
  197.0 135.8 %reduce-scatter.2.cloned.1.call-start = ((), (), s32[]{:S(2)}) async-start(), calls=%async_computation.4 | async-start | bytes 2228224 | tf_op jit(solution)/shard_map/reduce_scatter | solution.py:111
  257.0 2.7 copy-start.1
  263.6 0.7 copy-start.4
  364.2 25.5 %all-to-all-start = ((bf16[32,2,1024]{2,1,0:T(2,128)(2,1)}), bf16[32,2,1024]{2,1,0:T(2,128)(2,1)S(1)}, u32[]{:S(2)}, u32[]{:S(2)}) async-start(bf16[32,2,1024]{2,1,0:T(2,128)(2,1)} %reshape.120), calls=%async_computation.1 | async-start | bytes 262144 | tf_op jit(solution)/shard_map/all_to_all | solution.py:117
Sparse Core Ops, SparseCore 0:
  10.1 66.9 all-gather.2
  197.1 59.8 all-gather.4
  263.8 69.0 reduce-scatter.1
where the time goes:
time: 402 us; the launch traced here: 401 us
  blocking collectives  178 us (44%)
  waiting for transfers between devices  135 us (34%)
  other arithmetic  27.9 us (7%)
  starting transfers between devices  18.2 us (5%)
  local copies, waits for them, and re-layouts  16 us (4%)
  between operations  13.9 us (3%)
  matrix products  11.5 us (3%)
    reduce_scatter x1, waiting for transfers between devices, per_device(): lax.psum_scatter(expert_rows(rows_all, w_gate, w_up, w_down).astype(jnp.b...  68.4 us
    psum x1, blocking collectives, per_device(): sq_mean = lax.psum(jnp.sum(residual * residual, axis=1), 'exp') / D  62.2 us
    all_gather x1, waiting for transfers between devices, per_device(): rows_all = lax.all_gather(picked, 'ctx', axis=0, tiled=True)  59.8 us
    all_gather x1, blocking collectives, per_device(): attn_all = lax.all_gather(attn_local, 'exp', axis=1, tiled=True)  37.8 us
    all_gather x1, blocking collectives, per_device(): key_piece = lax.all_gather(key_part, 'ctx', axis=0, tiled=True)  31.5 us
    all_gather x1, blocking collectives, per_device(): full_rows = lax.all_gather(normed, 'exp', axis=1, tiled=True)  25 us
    unnamed x1, other arithmetic  23.4 us
    all_gather x1, blocking collectives, per_device(): value_piece = lax.all_gather(value_part, 'ctx', axis=0, tiled=True)  21.8 us
  transfers between devices with their start and end apart: 4, of which 3 were waited for; matrix products, arithmetic and copies ran while one was open for 2% of the time, Pallas kernels for 0%

commit v1 on v0

v1 whole, which is shorter than its diff:
```python
import math

import jax
import jax.numpy as jnp
from jax import lax
from jax.sharding import PartitionSpec as P

D = 4096
QUERY_HEAD_COUNT = 32
KEY_VALUE_HEADS = 8
HEAD_SIZE = 128
EXPERTS = 8
TOP = 2
CAP = 16
W_FIRST = 112


def three_terms(value):
    high = lax.reduce_precision(value, 8, 7)
    rest = value - high
    mid = lax.reduce_precision(rest, 8, 7)
    low = rest - mid
    return [part.astype(jnp.bfloat16) for part in (high, mid, low)]


def tie(value, other):
    return value + (other.reshape(-1)[0].astype(jnp.float32) * 0.0).astype(value.dtype)


def slot_index(own_route):
    seg_len = own_route.shape[0]
    experts = jnp.arange(EXPERTS, dtype=jnp.int32)
    named = (own_route[:, :, None] == experts[None, None, :]).astype(jnp.float32)
    rows = jnp.arange(seg_len, dtype=jnp.int32)
    before = (rows[None, :] < rows[:, None]).astype(jnp.bfloat16)
    earlier = jnp.dot(
        before, named.sum(axis=1).astype(jnp.bfloat16), preferred_element_type=jnp.float32
    )
    slot = jnp.sum(named * earlier[:, None, :], axis=2).astype(jnp.int32)
    return own_route * CAP + slot


def per_device(
    queries, keys, values, out_proj, residual_in, norm_gain, routes, gate_wts, w_gate, w_up, w_down
):
    ctx_count = lax.axis_size("ctx")
    exp_count = lax.axis_size("exp")
    ctx_rank = lax.axis_index("ctx")
    exp_rank = lax.axis_index("exp")
    seg_len = queries.shape[0]
    quarters = exp_count // EXPERTS
    rows_dev = CAP // quarters
    pair = [(i, i ^ 1) for i in range(exp_count)]
    chip = [(i, i ^ 2) for i in range(exp_count)]

    near = [w_gate, w_up, w_down]
    far = [lax.ppermute(w, "exp", chip) for w in near]

    kv_first = (exp_rank // (QUERY_HEAD_COUNT // KEY_VALUE_HEADS)) * HEAD_SIZE
    key_part = lax.dynamic_slice_in_dim(keys, kv_first, HEAD_SIZE, 1)
    value_part = lax.dynamic_slice_in_dim(values, kv_first, HEAD_SIZE, 1)
    first = lax.all_gather(
        jnp.concatenate([key_part, value_part, out_proj[:W_FIRST]], axis=0), "ctx", axis=0
    )
    key_all = first[:, :seg_len].reshape(ctx_count * seg_len, HEAD_SIZE)
    value_all = first[:, seg_len : 2 * seg_len].reshape(ctx_count * seg_len, HEAD_SIZE)

    scores = jnp.dot(queries, key_all.T, preferred_element_type=jnp.float32) * (
        1.0 / math.sqrt(HEAD_SIZE)
    )
    query_pos = ctx_rank * seg_len + jnp.arange(seg_len, dtype=jnp.int32)
    key_pos = jnp.arange(ctx_count * seg_len, dtype=jnp.int32)
    visible = query_pos[:, None] >= key_pos[None, :]
    scores = jnp.where(visible, scores, -1e30)
    weights = jnp.where(visible, jnp.exp(scores - jnp.max(scores, axis=1, keepdims=True)), 0.0)
    total = jnp.sum(weights, axis=1, keepdims=True)
    attn = jnp.dot(weights.astype(jnp.bfloat16), value_all, preferred_element_type=jnp.float32)
    attn_local = (attn / total).astype(jnp.bfloat16)

    gain_rows = jnp.stack(three_terms(norm_gain) + [jnp.zeros_like(norm_gain, jnp.bfloat16)] * 5)
    sent = jnp.concatenate([attn_local, gain_rows], axis=0)
    heads = lax.all_to_all(jnp.broadcast_to(sent[None], (exp_count,) + sent.shape), "exp", 0, 0)
    second = lax.all_gather(tie(out_proj[W_FIRST:], attn_local), "ctx", axis=0)
    attn_all = heads[:, :seg_len].transpose(1, 0, 2).reshape(seg_len, D)
    gain_all = heads[:, seg_len : seg_len + 3].astype(jnp.float32).sum(axis=1).reshape(1, D)
    proj = jnp.concatenate([first[:, 2 * seg_len :], second], axis=1).reshape(D, -1)

    residual = residual_in.astype(jnp.float32) + jnp.dot(
        attn_all, proj, preferred_element_type=jnp.float32
    )
    residual_out = residual.astype(jnp.bfloat16)

    own_route = lax.dynamic_slice_in_dim(routes, ctx_rank * seg_len, seg_len, 0)
    place = slot_index(own_route)
    slot_ids = jnp.arange(EXPERTS * CAP, dtype=jnp.int32)
    chosen = (place[:, :, None] == slot_ids[None, None, :]).astype(jnp.float32)
    picked = lax.dot_general(
        chosen.sum(axis=1).astype(jnp.bfloat16),
        residual_out,
        (((0,), (0,)), ((), ())),
        preferred_element_type=jnp.float32,
    ).astype(jnp.bfloat16)
    mine = lax.all_to_all(picked.reshape(exp_count, rows_dev, -1), "exp", 0, 0)
    mine = mine.transpose(1, 0, 2).reshape(rows_dev, D).astype(jnp.float32)
    sq_mean = jnp.mean(mine * mine, axis=1, keepdims=True)
    normed = (mine * lax.rsqrt(sq_mean + 1e-05) * gain_all).astype(jnp.bfloat16)
    rows_all = lax.all_gather(normed, "ctx", axis=0).reshape(ctx_count * rows_dev, D)

    across = [lax.ppermute(w, "exp", pair) for w in near]
    across_far = [lax.ppermute(w, "exp", pair) for w in far]
    out = jnp.zeros((ctx_count * rows_dev, D), jnp.float32)
    for gate_w, up_w, down_w in (near, across, far, across_far):
        gate_val = jnp.dot(rows_all, gate_w, preferred_element_type=jnp.float32)
        up_val = jnp.dot(rows_all, up_w, preferred_element_type=jnp.float32)
        hidden = (jax.nn.silu(gate_val) * up_val).astype(jnp.bfloat16)
        out = out + jnp.dot(hidden, down_w, preferred_element_type=jnp.float32)

    parts = lax.all_to_all(
        out.astype(jnp.bfloat16).reshape(ctx_count, rows_dev, D), "ctx", 0, 0
    )
    summed = parts.astype(jnp.float32).sum(axis=0).astype(jnp.bfloat16)
    back = lax.all_to_all(
        summed.reshape(rows_dev, exp_count, -1).transpose(1, 0, 2), "exp", 0, 0
    ).reshape(EXPERTS * CAP, -1)
    combine = jnp.sum(chosen * gate_wts[:, :, None], axis=1)
    expert_out = jnp.dot(
        combine, back.astype(jnp.float32), precision=lax.Precision.HIGHEST
    ).astype(jnp.bfloat16)
    return (residual_out, expert_out)


def solution(mesh):
    placed = (
        P("ctx", "exp"),
        P("ctx", None),
        P("ctx", None),
        P("ctx", "exp"),
        P("ctx", "exp"),
        P("exp"),
        P(),
        P("ctx", None),
        P(None, ("exp", "ctx")),
        P(None, ("exp", "ctx")),
        P(("exp", "ctx"), None),
    )
    return jax.shard_map(
        per_device,
        mesh=mesh,
        in_specs=placed,
        out_specs=(P("ctx", "exp"), P("ctx", "exp")),
        check_vma=False,
    )
```

time: 402 us -> 220 us (0.55)
  waiting for transfers between devices: 135 us -> 7.23 us
  blocking collectives: 178 us -> 123 us
  starting transfers between devices: 18.2 us -> 62.8 us
  other arithmetic: 27.9 us -> 1.76 us
  between operations: 13.9 us -> 1.72 us
  local copies, waits for them, and re-layouts: 16 us -> 4.77 us
  matrix products: 11.5 us -> 16.9 us
    reduce_scatter x1 -> x0, waiting for transfers between devices: 68.4 us -> none  [per_device(): lax.psum_scatter(expert_rows(rows_all, w_gate, w_up, w_down).astype(jnp.b...]
    psum x1 -> x0, blocking collectives: 62.2 us -> none  [per_device(): sq_mean = lax.psum(jnp.sum(residual * residual, axis=1), 'exp') / D]
    all_gather x2 -> x0, waiting for transfers between devices: 59.8 us -> none  [the longest x1 59.8 us: per_device(): rows_all = lax.all_gather(picked, 'ctx', axis=0, tiled=True)]
    all_to_all x0 -> x2, blocking collectives: none -> 47.1 us  [the longest x1 29.7 us: per_device(): lax.all_to_all(out.astype(jnp.bfloat16).reshape(ctx_count, rows_dev, D),...]
    all_gather x4 -> x3, blocking collectives: 116 us -> 76.2 us  [the longest x1 29.4 us: per_device(): lax.all_gather(jnp.concatenate([key_part, value_part, out_proj[:W_FIRST]]...]
    ppermute x0 -> x9, starting transfers between devices: none -> 35.1 us  [the longest x3 20 us: per_device(): across = [lax.ppermute(w, 'exp', pair) for w in near]]
    unnamed x1 -> x0, other arithmetic: 23.4 us -> none
    all_to_all x1 -> x2, starting transfers between devices: 17.9 us -> 27.7 us  [the longest x1 14 us: per_device(): lax.all_to_all(jnp.broadcast_to(sent[None], (exp_count,) + sent.shape), '...]
  transfers between devices with their start and end apart: 4 -> 11, of which waited for: 3 -> 1; matrix products, arithmetic and copies ran while one was open for 2% -> 9% of each run, Pallas kernels for 0% -> 0%
where the time goes in v1:
time: 220 us; the launch traced here: 219 us
  blocking collectives  123 us (56%)
  starting transfers between devices  62.8 us (29%)
  matrix products  16.9 us (8%)
  waiting for transfers between devices  7.23 us (3%)
  local copies, waits for them, and re-layouts  4.77 us (2%)
    all_to_all x1, blocking collectives, per_device(): lax.all_to_all(out.astype(jnp.bfloat16).reshape(ctx_count, rows_dev, D),...  29.7 us
    all_gather x1, blocking collectives, per_device(): lax.all_gather(jnp.concatenate([key_part, value_part, out_proj[:W_FIRST]]...  29.4 us
    all_gather x1, blocking collectives, per_device(): lax.all_gather(normed, 'ctx', axis=0).reshape(ctx_count * rows_dev, D)  24 us
    all_gather x1, blocking collectives, per_device(): second = lax.all_gather(tie(out_proj[W_FIRST:], attn_local), 'ctx', axis=0)  22.8 us
    ppermute x3, starting transfers between devices, per_device(): across = [lax.ppermute(w, 'exp', pair) for w in near]  20 us
    all_to_all x1, blocking collectives, per_device(): lax.all_to_all(summed.reshape(rows_dev, exp_count, -1).transpose(1, 0, 2)...  17.4 us
    all_to_all x1, starting transfers between devices, per_device(): lax.all_to_all(jnp.broadcast_to(sent[None], (exp_count,) + sent.shape), '...  14 us
    all_to_all x1, starting transfers between devices, per_device(): mine = lax.all_to_all(picked.reshape(exp_count, rows_dev, -1), 'exp', 0, 0)  13.7 us
  transfers between devices with their start and end apart: 11, of which 1 were waited for; matrix products, arithmetic and copies ran while one was open for 9% of the time, Pallas kernels for 0%

profile of v1, /device:TPU:1, one launch (start us, length us, event | category | flops | bytes accessed | tf_op | source)
XLA Modules:
  0.0 218.5 jit_solution(12731579383790782654)
XLA Ops:
  0.6 0.0 copy-start
  0.6 8.8 %collective-permute-start.2 = (bf16[128,4096]{1,0:T(8,128)(2,1)}, bf16[128,4096]{1,0:T(8,128)(2,1)}, u32[]{:S(2)}, u32[]{:S(2)}) collective-permute-start(bf16[128,4096]{1,0:T(8,128)(2,1)} %param.21), channel_id=1, source_target_pairs={{0,1},{1,0},{2,3},{3,2},{4,5},{5,4},{6,7},{7,6},{8,9},{9,8},{10,11... | collective-permute-start | bytes 3145736 | tf_op jit(solution)/shard_map/ppermute | solution.py:109
  9.4 1.9 collective-permute-start.5
  11.4 1.9 collective-permute-start
  13.3 3.6 %collective-permute-start.3 = (bf16[4096,128]{1,0:T(8,128)(2,1)}, bf16[4096,128]{1,0:T(8,128)(2,1)}, u32[]{:S(2)}, u32[]{:S(2)}) collective-permute-start(bf16[4096,128]{1,0:T(8,128)(2,1)} %param.19), channel_id=1, source_target_pairs={{0,2},{1,3},{2,0},{3,1},{4,6},{5,7},{6,4},{7,5},{8,10},{9,11},{10,... | collective-permute-start | bytes 3145736 | tf_op jit(solution)/shard_map/ppermute | solution.py:57
  17.0 0.8 slice.24
  17.7 0.7 constant_dynamic-slice_fusion.1
  18.5 0.0 copy-start.5
  18.5 29.4 %all-gather = bf16[3840,128]{1,0:T(8,128)(2,1)S(1)} all-gather(bf16[240,128]{1,0:T(8,128)(2,1)S(1)} %pad_maximum_fusion.1), channel_id=2, replica_groups=mesh['ctx'=16,'exp'=32] {'ctx'}, dimensions={0}, use_global_device_ids=true | all-gather | bytes 1044480 | tf_op jit(solution)/shard_map/all_gather | solution.py:62
  47.9 0.1 fusion.40
  48.0 0.0 copy-done.5
  48.0 0.0 copy-done
  48.0 0.3 fusion.41
  48.3 0.2 fusion.9
  48.5 0.2 fusion.5
  48.8 0.0 copy-start.2
  48.9 0.9 broadcast_in_dim.11
  49.8 14.0 %all-to-all-start = ((bf16[32,72,128]{2,1,0:T(8,128)(2,1)}), bf16[32,72,128]{2,1,0:T(8,128)(2,1)S(1)}, u32[]{:S(2)}, u32[]{:S(2)}) async-start(bf16[32,72,128]{2,1,0:T(8,128)(2,1)} %broadcast_in_dim.11), calls=%async_computation | async-start | bytes 1179648 | tf_op jit(solution)/shard_map/all_to_all | solution.py:82
  63.8 3.3 %collective-permute-start.4 = (bf16[4096,128]{1,0:T(8,128)(2,1)}, bf16[4096,128]{1,0:T(8,128)(2,1)}, u32[]{:S(2)}, u32[]{:S(2)}) collective-permute-start(bf16[4096,128]{1,0:T(8,128)(2,1)} %param.20), channel_id=1, source_target_pairs={{0,2},{1,3},{2,0},{3,1},{4,6},{5,7},{6,4},{7,5},{8,10},{9,11},{10,... | collective-permute-start | bytes 3145736 | tf_op jit(solution)/shard_map/ppermute | solution.py:57
  67.1 0.5 slice.36
  68.3 0.8 constant_dynamic-slice_fusion
  69.1 0.1 fusion.24
  69.2 0.8 convert_add_fusion
  70.1 0.1 convert_reduce_fusion.1
  70.2 22.8 %all-gather.1 = bf16[2304,128]{1,0:T(8,128)(2,1)S(1)} all-gather(bf16[144,128]{1,0:T(8,128)(2,1)S(1)} %slice_add_fusion), channel_id=3, replica_groups=mesh['ctx'=16,'exp'=32] {'ctx'}, dimensions={0}, use_global_device_ids=true | all-gather | bytes 626688 | tf_op jit(solution)/shard_map/all_gather | solution.py:83
  92.9 0.1 pad_maximum_fusion
  93.0 0.0 all-to-all-done
  93.0 0.6 copy-done.6
  93.6 0.3 fusion.3
  94.0 0.0 copy-start.3
  94.0 0.8 convolution_convert_fusion
  94.8 13.7 %all-to-all-start.1 = ((bf16[32,4,128]{2,1,0:T(4,128)(2,1)}), bf16[32,4,128]{2,1,0:T(4,128)(2,1)S(1)}, u32[]{:S(2)}, u32[]{:S(2)}) async-start(bf16[32,4,128]{2,1,0:T(4,128)(2,1)} %bitcast.12), calls=%async_computation.1 | async-start | bytes 65536 | tf_op jit(solution)/shard_map/all_to_all | solution.py:103
  108.5 7.2 %all-to-all-done.1 = bf16[32,4,128]{2,1,0:T(4,128)(2,1)S(1)} async-done(((bf16[32,4,128]{2,1,0:T(4,128)(2,1)}), bf16[32,4,128]{2,1,0:T(4,128)(2,1)S(1)}, u32[]{:S(2)}, u32[]{:S(2)}) %all-to-all-start.1) | async-done | bytes 32800 | tf_op jit(solution)/shard_map/all_to_all | solution.py:103
  115.7 0.1 fusion.18
  115.9 0.1 fusion.17
  116.0 24.0 %all_gather.20 = bf16[16,4,4096]{2,1,0:T(4,128)(2,1)S(1)} all-gather(bf16[1,4,4096]{2,1,0:T(4,128)(2,1)S(1)} %fusion.17), channel_id=1, replica_groups=mesh['ctx'=16,'exp'=32] {'ctx'}, dimensions={0}, use_global_device_ids=true | all-gather | bytes 557056 | tf_op jit(solution)/shard_map/all_gather | solution.py:107
  140.0 0.1 reshape.130
  140.1 0.0 copy-start.1
  140.1 0.0 collective-permute-done
  140.1 9.3 %collective-permute-start.1 = (bf16[4096,128]{1,0:T(8,128)(2,1)}, bf16[4096,128]{1,0:T(8,128)(2,1)}, u32[]{:S(2)}, u32[]{:S(2)}) collective-permute-start(bf16[4096,128]{1,0:T(8,128)(2,1)} %param.20), channel_id=1, source_target_pairs={{0,1},{1,0},{2,3},{3,2},{4,5},{5,4},{6,7},{7,6},{8,9},{9,8},{10,11... | collective-permute-start | bytes 3145736 | tf_op jit(solution)/shard_map/ppermute | solution.py:109
  149.4 1.5 fusion.48
  151.0 1.8 fusion.6
  152.8 0.0 collective-permute-done.3
  152.8 1.9 collective-permute-start.6
  154.8 1.5 fusion.50
  156.3 0.0 collective-permute-done.5
  156.3 2.4 %collective-permute-start.8 = (bf16[128,4096]{1,0:T(8,128)(2,1)}, bf16[128,4096]{1,0:T(8,128)(2,1)}, u32[]{:S(2)}, u32[]{:S(2)}) collective-permute-start(bf16[128,4096]{1,0:T(8,128)(2,1)} %collective-permute-done.5), channel_id=1, source_target_pairs={{0,1},{1,0},{2,3},{3,2},{4,5},{5,4},{6,7},{7,6},{8,9},{9,8},{10,11... | collective-permute-start | bytes 3145736 | tf_op jit(solution)/shard_map/ppermute | solution.py:110
  158.7 0.0 collective-permute-done.4
  158.7 1.9 collective-permute-start.7
  160.7 1.5 fusion.49
  162.2 0.0 collective-permute-done.2
  162.2 0.0 collective-permute-done.1
  162.2 2.1 convolution_add_fusion.2
  164.4 2.1 convolution_add_fusion.1
  166.5 0.0 collective-permute-done.6
  166.5 1.5 fusion.51
  168.1 0.0 collective-permute-done.8
  168.1 0.0 collective-permute-done.7
  168.1 2.1 fusion
  170.2 0.2 reshape.131
  170.4 29.7 %all_to_all.20 = bf16[16,4,4096]{2,1,0:T(4,128)(2,1)S(1)} all-to-all(bf16[16,4,4096]{2,1,0:T(4,128)(2,1)S(1)} %reshape.131), channel_id=1, replica_groups=mesh['ctx'=16,'exp'=32] {'ctx'}, dimensions={0} | all-to-all | bytes 1048576 | tf_op jit(solution)/shard_map/all_to_all | solution.py:118
  200.1 0.2 reduce_sum.82
  200.4 17.4 %all_to_all.21 = bf16[32,4,128]{2,1,0:T(4,128)(2,1)S(1)} all-to-all(bf16[32,4,128]{2,1,0:T(4,128)(2,1)S(1)} %bitcast.76), channel_id=1, replica_groups=mesh['ctx'=16,'exp'=32] {'exp'}, dimensions={0} | all-to-all | bytes 65536 | tf_op jit(solution)/shard_map/all_to_all | solution.py:122
  217.8 0.8 convolution_convert_fusion.1
  (18 shorter events, 0.2 us)
Async XLA Ops:
  0.6 47.4 %copy-start = (bf16[64,128]{1,0:T(8,128)(2,1)S(1)}, bf16[64,128]{1,0:T(8,128)(2,1)}, u32[]{:S(2)}) copy-start(bf16[64,128]{1,0:T(8,128)(2,1)} %param.11) | copy-start | bytes 49156
  0.6 161.6 %collective-permute-start.2 = (bf16[128,4096]{1,0:T(8,128)(2,1)}, bf16[128,4096]{1,0:T(8,128)(2,1)}, u32[]{:S(2)}, u32[]{:S(2)}) collective-permute-start(bf16[128,4096]{1,0:T(8,128)(2,1)} %param.21), channel_id=1, source_target_pairs={{0,1},{1,0},{2,3},{3,2},{4,5},{5,4},{6,7},{7,6},{8,9},{9,8},{10,11... | collective-permute-start | bytes 3145736 | tf_op jit(solution)/shard_map/ppermute | solution.py:109
  9.4 146.9 %collective-permute-start.5 = (bf16[128,4096]{1,0:T(8,128)(2,1)}, bf16[128,4096]{1,0:T(8,128)(2,1)}, u32[]{:S(2)}, u32[]{:S(2)}) collective-permute-start(bf16[128,4096]{1,0:T(8,128)(2,1)} %param.21), channel_id=1, source_target_pairs={{0,2},{1,3},{2,0},{3,1},{4,6},{5,7},{6,4},{7,5},{8,10},{9,11},{10,... | collective-permute-start | bytes 3145736 | tf_op jit(solution)/shard_map/ppermute | solution.py:57
  11.4 128.8 %collective-permute-start = (bf16[4096,128]{1,0:T(8,128)(2,1)}, bf16[4096,128]{1,0:T(8,128)(2,1)}, u32[]{:S(2)}, u32[]{:S(2)}) collective-permute-start(bf16[4096,128]{1,0:T(8,128)(2,1)} %param.19), channel_id=1, source_target_pairs={{0,1},{1,0},{2,3},{3,2},{4,5},{5,4},{6,7},{7,6},{8,9},{9,8},{10,11... | collective-permute-start | bytes 3145736 | tf_op jit(solution)/shard_map/ppermute | solution.py:109
  13.3 139.5 %collective-permute-start.3 = (bf16[4096,128]{1,0:T(8,128)(2,1)}, bf16[4096,128]{1,0:T(8,128)(2,1)}, u32[]{:S(2)}, u32[]{:S(2)}) collective-permute-start(bf16[4096,128]{1,0:T(8,128)(2,1)} %param.19), channel_id=1, source_target_pairs={{0,2},{1,3},{2,0},{3,1},{4,6},{5,7},{6,4},{7,5},{8,10},{9,11},{10,... | collective-permute-start | bytes 3145736 | tf_op jit(solution)/shard_map/ppermute | solution.py:57
  18.5 29.5 %copy-start.5 = (f32[128]{0:T(128)S(1)}, f32[128]{0:T(128)}, u32[]{:S(2)}) copy-start(f32[128]{0:T(128)} %param.16) | copy-start | bytes 1540
  48.8 19.5 %copy-start.2 = (bf16[256,128]{1,0:T(8,128)(2,1)S(1)}, bf16[256,128]{1,0:T(8,128)(2,1)}, u32[]{:S(2)}) copy-start(bf16[256,128]{1,0:T(8,128)(2,1)} %param.14) | copy-start | bytes 196612
  49.8 20.3 %copy-start.4 = (f32[64,2]{0,1:T(2,128)S(1)}, f32[64,2]{0,1:T(2,128)}, u32[]{:S(2)}) copy-start(f32[64,2]{0,1:T(2,128)} %param.18) | copy-start | bytes 1540
  49.8 43.3 %all-to-all-start = ((bf16[32,72,128]{2,1,0:T(8,128)(2,1)}), bf16[32,72,128]{2,1,0:T(8,128)(2,1)S(1)}, u32[]{:S(2)}, u32[]{:S(2)}) async-start(bf16[32,72,128]{2,1,0:T(8,128)(2,1)} %broadcast_in_dim.11), calls=%async_computation | async-start | bytes 1179648 | tf_op jit(solution)/shard_map/all_to_all | solution.py:82
  63.8 94.9 %collective-permute-start.4 = (bf16[4096,128]{1,0:T(8,128)(2,1)}, bf16[4096,128]{1,0:T(8,128)(2,1)}, u32[]{:S(2)}, u32[]{:S(2)}) collective-permute-start(bf16[4096,128]{1,0:T(8,128)(2,1)} %param.20), channel_id=1, source_target_pairs={{0,2},{1,3},{2,0},{3,1},{4,6},{5,7},{6,4},{7,5},{8,10},{9,11},{10,... | collective-permute-start | bytes 3145736 | tf_op jit(solution)/shard_map/ppermute | solution.py:57
  92.9 0.7 copy-start.6
  94.0 57.0 %copy-start.3 = (bf16[64,128]{1,0:T(8,128)(2,1)}, bf16[64,128]{1,0:T(8,128)(2,1)S(1)}, u32[]{:S(2)}) copy-start(bf16[64,128]{1,0:T(8,128)(2,1)S(1)} %fusion.3) | copy-start | bytes 49156
  94.8 20.9 %all-to-all-start.1 = ((bf16[32,4,128]{2,1,0:T(4,128)(2,1)}), bf16[32,4,128]{2,1,0:T(4,128)(2,1)S(1)}, u32[]{:S(2)}, u32[]{:S(2)}) async-start(bf16[32,4,128]{2,1,0:T(4,128)(2,1)} %bitcast.12), calls=%async_computation.1 | async-start | bytes 65536 | tf_op jit(solution)/shard_map/all_to_all | solution.py:103
  140.1 10.9 %copy-start.1 = (bf16[128,4096]{1,0:T(8,128)(2,1)S(1)}, bf16[128,4096]{1,0:T(8,128)(2,1)}, u32[]{:S(2)}) copy-start(bf16[128,4096]{1,0:T(8,128)(2,1)} %param.21) | copy-start | bytes 3145732
  140.1 22.1 %collective-permute-start.1 = (bf16[4096,128]{1,0:T(8,128)(2,1)}, bf16[4096,128]{1,0:T(8,128)(2,1)}, u32[]{:S(2)}, u32[]{:S(2)}) collective-permute-start(bf16[4096,128]{1,0:T(8,128)(2,1)} %param.20), channel_id=1, source_target_pairs={{0,1},{1,0},{2,3},{3,2},{4,5},{5,4},{6,7},{7,6},{8,9},{9,8},{10,11... | collective-permute-start | bytes 3145736 | tf_op jit(solution)/shard_map/ppermute | solution.py:109
  152.8 13.7 %collective-permute-start.6 = (bf16[4096,128]{1,0:T(8,128)(2,1)}, bf16[4096,128]{1,0:T(8,128)(2,1)}, u32[]{:S(2)}, u32[]{:S(2)}) collective-permute-start(bf16[4096,128]{1,0:T(8,128)(2,1)} %collective-permute-done.3), channel_id=1, source_target_pairs={{0,1},{1,0},{2,3},{3,2},{4,5},{5,4},{6,7},{7,6},{8,9},{9,8},{10,11... | collective-permute-start | bytes 3145736 | tf_op jit(solution)/shard_map/ppermute | solution.py:110
  156.3 11.7 %collective-permute-start.8 = (bf16[128,4096]{1,0:T(8,128)(2,1)}, bf16[128,4096]{1,0:T(8,128)(2,1)}, u32[]{:S(2)}, u32[]{:S(2)}) collective-permute-start(bf16[128,4096]{1,0:T(8,128)(2,1)} %collective-permute-done.5), channel_id=1, source_target_pairs={{0,1},{1,0},{2,3},{3,2},{4,5},{5,4},{6,7},{7,6},{8,9},{9,8},{10,11... | collective-permute-start | bytes 3145736 | tf_op jit(solution)/shard_map/ppermute | solution.py:110
  158.7 9.3 %collective-permute-start.7 = (bf16[4096,128]{1,0:T(8,128)(2,1)}, bf16[4096,128]{1,0:T(8,128)(2,1)}, u32[]{:S(2)}, u32[]{:S(2)}) collective-permute-start(bf16[4096,128]{1,0:T(8,128)(2,1)} %collective-permute-done.4), channel_id=1, source_target_pairs={{0,1},{1,0},{2,3},{3,2},{4,5},{5,4},{6,7},{7,6},{8,9},{9,8},{10,11... | collective-permute-start | bytes 3145736 | tf_op jit(solution)/shard_map/ppermute | solution.py:110

commit v2 on v1

v2 whole, which is shorter than its diff:
```python
import math

import jax
import jax.numpy as jnp
from jax import lax
from jax.experimental import pallas as pl
from jax.experimental.pallas import tpu as pltpu
from jax.sharding import PartitionSpec as P

D = 4096
QUERY_HEAD_COUNT = 32
KEY_VALUE_HEADS = 8
HEAD_SIZE = 128
EXPERTS = 8
TOP = 2
CAP = 16
SEG = 64
SHARDS = 16
W_FIRST = 112
EXTRA = 16

VMEM = pl.BlockSpec(memory_space=pltpu.VMEM)
SMEM = pl.BlockSpec(memory_space=pltpu.SMEM)
ANY = pl.BlockSpec(memory_space=pl.ANY)
ATTENTION_ROOM = 16 * 1024 * 1024
ROOM = 63 * 1024 * 1024 - 512 * 1024
F32 = jnp.float32
BF16 = jnp.bfloat16


def three_terms(value):
    high = value.astype(BF16)
    rest = value - high.astype(F32)
    mid = rest.astype(BF16)
    return [high, mid, (rest - mid.astype(F32)).astype(BF16)]


def slot_places(routes):
    seg_len = routes.shape[1]
    experts = jnp.arange(EXPERTS, dtype=jnp.int32)
    named = (routes[:, :, :, None] == experts).astype(F32)
    rows = jnp.arange(seg_len, dtype=jnp.int32)
    before = (rows[None, :] < rows[:, None]).astype(BF16)
    earlier = jnp.einsum(
        "ts,cse->cte", before, named.sum(axis=2).astype(BF16), preferred_element_type=F32
    )
    slot = jnp.sum(named * earlier[:, :, None, :], axis=3).astype(jnp.int32)
    return routes * CAP + slot


def pack_kernel(
    head_ref, gate_ref, up_ref, down_ref, key_ref, value_ref, proj_ref,
    out_ref, first_ref, gate_v, up_v, down_v, packed_v, sems,
):
    column = pl.ds(pl.multiple_of(head_ref[0] * HEAD_SIZE, HEAD_SIZE), HEAD_SIZE)
    copies = [
        pltpu.make_async_copy(src, dst, sems.at[i])
        for i, (src, dst) in enumerate(
            (
                (down_ref, down_v),
                (gate_ref, gate_v),
                (up_ref, up_v),
                (key_ref.at[:, column], first_ref.at[pl.ds(0, SEG)]),
                (value_ref.at[:, column], first_ref.at[pl.ds(SEG, SEG)]),
                (proj_ref.at[pl.ds(0, W_FIRST)], first_ref.at[pl.ds(2 * SEG, W_FIRST)]),
            )
        )
    ]
    for copy in copies:
        copy.start()
    outs = [
        pltpu.make_async_copy(src, out_ref.at[pl.ds(i * D, D)], sems.at[6 + i])
        for i, src in enumerate((gate_v, up_v, packed_v))
    ]
    copies[0].wait()
    for b in range(D // 128):
        packed_v[b * 128 : (b + 1) * 128] = down_v[:, b * 128 : (b + 1) * 128]
    outs[2].start()
    copies[1].wait()
    outs[0].start()
    copies[2].wait()
    outs[1].start()
    for copy in copies[3:] + outs:
        copy.wait()


def pack(head, w_gate, w_up, w_down, keys, values, out_proj):
    return pl.pallas_call(
        pack_kernel,
        out_shape=[
            jax.ShapeDtypeStruct((3 * D, 128), BF16),
            jax.ShapeDtypeStruct((2 * SEG + W_FIRST, HEAD_SIZE), BF16),
        ],
        in_specs=[SMEM] + [ANY] * 6,
        out_specs=[ANY, VMEM],
        scratch_shapes=[
            pltpu.VMEM((D, 128), BF16),
            pltpu.VMEM((D, 128), BF16),
            pltpu.VMEM((128, D), BF16),
            pltpu.VMEM((D, 128), BF16),
            pltpu.SemaphoreType.DMA((9,)),
        ],
        compiler_params=pltpu.CompilerParams(vmem_limit_bytes=ROOM),
    )(head, w_gate, w_up, w_down, keys, values, out_proj)


def attention_kernel(
    ctx_ref, query_ref, first_ref, gain_ref, gate_ref, proj_ref, out_ref, second_ref
):
    second_ref[: proj_ref.shape[0] - W_FIRST] = proj_ref[W_FIRST:]
    second_ref[proj_ref.shape[0] - W_FIRST :] = gate_ref[...]
    count = SHARDS * SEG
    key_all = first_ref[:, :SEG].reshape(count, HEAD_SIZE)
    value_all = first_ref[:, SEG : 2 * SEG].reshape(count, HEAD_SIZE)
    scores = lax.dot_general(
        query_ref[...], key_all, (((1,), (1,)), ((), ())), preferred_element_type=F32
    ) * (1.0 / math.sqrt(HEAD_SIZE))
    row = lax.broadcasted_iota(jnp.int32, scores.shape, 0) + ctx_ref[0] * SEG
    visible = row >= lax.broadcasted_iota(jnp.int32, scores.shape, 1)
    scores = jnp.where(visible, scores, -1e30)
    weights = jnp.where(visible, jnp.exp(scores - jnp.max(scores, axis=1, keepdims=True)), 0.0)
    total = jnp.sum(weights, axis=1, keepdims=True)
    attn = jnp.dot(weights.astype(BF16), value_all, preferred_element_type=F32)
    gains = three_terms(jnp.broadcast_to(gain_ref[...], (EXTRA, HEAD_SIZE)))
    line = lax.broadcasted_iota(jnp.int32, (EXTRA, HEAD_SIZE), 0)
    gain_rows = jnp.zeros((EXTRA, HEAD_SIZE), F32)
    for k in range(3):
        gain_rows = jnp.where(line == k, gains[k].astype(F32), gain_rows)
    sent = jnp.concatenate([(attn / total).astype(BF16), gain_rows.astype(BF16)], axis=0)
    out_ref[...] = jnp.broadcast_to(sent[None], out_ref.shape)


def attention(ctx_rank, queries, first, gain, gate_rows, out_proj):
    return pl.pallas_call(
        attention_kernel,
        out_shape=[
            jax.ShapeDtypeStruct((QUERY_HEAD_COUNT, SEG + EXTRA, HEAD_SIZE), BF16),
            jax.ShapeDtypeStruct((out_proj.shape[0] - W_FIRST + EXTRA, HEAD_SIZE), BF16),
        ],
        in_specs=[SMEM] + [VMEM] * 5,
        out_specs=[VMEM, VMEM],
        compiler_params=pltpu.CompilerParams(vmem_limit_bytes=ATTENTION_ROOM),
    )(ctx_rank, queries, first, gain, gate_rows, out_proj)


def project_kernel(
    heads_ref, first_ref, second_ref, residual_ref, chosen_ref, near_ref, far_ref,
    out_ref, picked_ref, gain_ref, near_out, far_out, attn_v, proj_v,
):
    del near_ref, far_ref, near_out, far_out
    for h in range(QUERY_HEAD_COUNT):
        attn_v[:, h * 128 : (h + 1) * 128] = heads_ref[h, :SEG]
        gain_ref[:, h * 128 : (h + 1) * 128] = jnp.sum(
            heads_ref[h, SEG:].astype(F32), axis=0, keepdims=True
        )
    for c in range(SHARDS):
        proj_v[c * 256 : c * 256 + W_FIRST] = first_ref[c, 2 * SEG : 2 * SEG + W_FIRST]
        proj_v[c * 256 + W_FIRST : (c + 1) * 256] = second_ref[c, : 256 - W_FIRST]
    residual = residual_ref[...].astype(F32) + jnp.dot(
        attn_v[...], proj_v[...], preferred_element_type=F32
    )
    rounded = residual.astype(BF16)
    out_ref[...] = rounded
    picked_ref[...] = jnp.dot(
        chosen_ref[...], rounded, preferred_element_type=F32
    ).astype(BF16)


def project(heads, first, second, residual_in, chosen, near, far):
    return pl.pallas_call(
        project_kernel,
        out_shape=[
            jax.ShapeDtypeStruct((SEG, 128), BF16),
            jax.ShapeDtypeStruct((EXPERTS * CAP, 128), BF16),
            jax.ShapeDtypeStruct((1, D), F32),
            jax.ShapeDtypeStruct(near.shape, near.dtype),
            jax.ShapeDtypeStruct(far.shape, far.dtype),
        ],
        in_specs=[VMEM] * 5 + [ANY] * 2,
        out_specs=[VMEM] * 3 + [ANY] * 2,
        scratch_shapes=[pltpu.VMEM((SEG, D), BF16), pltpu.VMEM((D, 128), BF16)],
        input_output_aliases={5: 3, 6: 4},
        compiler_params=pltpu.CompilerParams(vmem_limit_bytes=ROOM),
    )(heads, first, second, residual_in, chosen, near, far)


def experts_kernel(x_ref, *refs):
    weights, (out_ref, held_v, hidden_v, sems) = refs[:4], refs[4:]
    copies = []
    for part in range(2):
        for i in range(4):
            rows = pl.ds(part * 2 * D, 2 * D if part == 0 else D)
            copies.append(
                pltpu.make_async_copy(weights[i].at[rows], held_v.at[i, rows], sems.at[i, part])
            )
    for copy in copies:
        copy.start()
    x = jnp.concatenate([x_ref[c].astype(F32) for c in range(SHARDS)], axis=0).astype(BF16)
    for i in range(4):
        copies[i].wait()
        both = jnp.dot(
            x,
            jnp.concatenate([held_v[i, :D], held_v[i, D : 2 * D]], axis=1),
            preferred_element_type=F32,
        )
        gate_val, up_val = both[:, :128], both[:, 128:]
        hidden_v[:, i * 128 : (i + 1) * 128] = (
            gate_val / (1.0 + jnp.exp(-gate_val)) * up_val
        ).astype(BF16)
    for i in range(4):
        copies[4 + i].wait()
    hidden = hidden_v[...]
    for b in range(0, D // 128, 2):
        start = 2 * D + b * 128
        down = jnp.concatenate(
            [
                jnp.concatenate(
                    [held_v[i, start : start + 128], held_v[i, start + 128 : start + 256]], axis=1
                )
                for i in range(4)
            ],
            axis=0,
        )
        part = jnp.dot(hidden, down, preferred_element_type=F32).astype(BF16)
        out_ref[b] = part[:, :128]
        out_ref[b + 1] = part[:, 128:]


def run_experts(rows_all, weights):
    rows = rows_all.shape[0] * rows_all.shape[1]
    return pl.pallas_call(
        experts_kernel,
        out_shape=jax.ShapeDtypeStruct((D // 128, rows, 128), BF16),
        in_specs=[VMEM] + [ANY] * 4,
        out_specs=VMEM,
        scratch_shapes=[
            pltpu.VMEM((4, 3 * D, 128), BF16),
            pltpu.VMEM((rows, 512), BF16),
            pltpu.SemaphoreType.DMA((4, 2)),
        ],
        compiler_params=pltpu.CompilerParams(vmem_limit_bytes=ROOM),
        cost_estimate=pl.CostEstimate(
            flops=2 * rows * 512 * D * 3, bytes_accessed=12 * 128 * D * 2, transcendentals=0
        ),
    )(rows_all, *weights)


def weigh_kernel(parts_ref, combine_ref, out_ref):
    for g in range(SHARDS // 4):
        rows = parts_ref[:, g * 16 : (g + 1) * 16].reshape(QUERY_HEAD_COUNT * 16, 128)
        total = jnp.dot(combine_ref[g], rows, preferred_element_type=F32)
        out_ref[g * 4 : (g + 1) * 4] = total.astype(BF16).reshape(4, SEG, 128)


def weigh(parts, combine):
    return pl.pallas_call(
        weigh_kernel,
        out_shape=jax.ShapeDtypeStruct((SHARDS, SEG, 128), BF16),
        in_specs=[VMEM] * 2,
        out_specs=VMEM,
        compiler_params=pltpu.CompilerParams(vmem_limit_bytes=16 * 1024 * 1024),
    )(parts, combine)


def per_device(
    queries, keys, values, out_proj, residual_in, norm_gain, routes, gate_wts, w_gate, w_up, w_down
):
    ctx_count = lax.axis_size("ctx")
    exp_count = lax.axis_size("exp")
    ctx_rank = lax.axis_index("ctx")
    exp_rank = lax.axis_index("exp")
    rows_dev = CAP // (exp_count // EXPERTS)
    pair = [(i, i ^ 1) for i in range(exp_count)]
    chip = [(i, i ^ 2) for i in range(exp_count)]

    head = (exp_rank // (QUERY_HEAD_COUNT // KEY_VALUE_HEADS)).astype(jnp.int32).reshape(1)
    near, sent = pack(head, w_gate, w_up, w_down, keys, values, out_proj)
    far = lax.ppermute(near, "exp", chip)

    first = lax.all_gather(sent, "ctx", axis=0)
    gate_row = gate_wts.T.reshape(1, TOP * SEG).astype(BF16)
    spread, rest = attention(
        ctx_rank.astype(jnp.int32).reshape(1),
        queries,
        first,
        norm_gain.reshape(1, -1),
        jnp.concatenate([gate_row, jnp.zeros((EXTRA - 1, TOP * SEG), BF16)], axis=0),
        out_proj,
    )
    heads = lax.all_to_all(spread, "exp", 0, 0)
    second = lax.all_gather(rest, "ctx", axis=0)
    gate_all = second[:, -EXTRA].reshape(ctx_count, TOP, SEG)

    place = slot_places(routes.reshape(ctx_count, SEG, TOP))
    own_place = lax.dynamic_index_in_dim(place, ctx_rank, 0, keepdims=False)
    slot_ids = jnp.arange(EXPERTS * CAP, dtype=jnp.int32)
    chosen = (own_place.T[:, None, :] == slot_ids[None, :, None]).astype(F32).sum(axis=0)
    shard = jnp.arange(ctx_count, dtype=jnp.int32)[:, None, None] % 4
    column = (place // rows_dev) * 16 + shard * rows_dev + place % rows_dev
    columns = jnp.arange(exp_count * 16, dtype=jnp.int32)
    combine = sum(
        jnp.where(column[:, :, k, None] == columns, gate_all[:, k, :, None], jnp.zeros((), BF16))
        for k in range(TOP)
    ).reshape(ctx_count // 4, 4 * SEG, exp_count * 16)

    residual_out, picked, gain_all, near, far = project(
        heads, first, second, residual_in, chosen.astype(BF16), near, far
    )
    across = lax.ppermute(near, "exp", pair)
    across_far = lax.ppermute(far, "exp", pair)

    mine = lax.all_to_all(picked.reshape(exp_count, rows_dev, -1), "exp", 0, 0)
    mine = mine.transpose(1, 0, 2).reshape(rows_dev, D).astype(F32)
    sq_mean = jnp.mean(mine * mine, axis=1, keepdims=True)
    normed = (mine * lax.rsqrt(sq_mean + 1e-05) * gain_all).astype(BF16)
    rows_all = lax.all_gather(normed, "ctx", axis=0)

    out = run_experts(rows_all, [near, across, far, across_far])

    parts = lax.all_to_all(out, "exp", 0, 0)
    pieces = lax.all_to_all(weigh(parts, combine), "ctx", 0, 0)
    expert_out = pieces.astype(F32).sum(axis=0).astype(BF16)
    return (residual_out, expert_out)


def solution(mesh):
    placed = (
        P("ctx", "exp"),
        P("ctx", None),
        P("ctx", None),
        P("ctx", "exp"),
        P("ctx", "exp"),
        P("exp"),
        P(),
        P("ctx", None),
        P(None, ("exp", "ctx")),
        P(None, ("exp", "ctx")),
        P(("exp", "ctx"), None),
    )
    return jax.shard_map(
        per_device,
        mesh=mesh,
        in_specs=placed,
        out_specs=(P("ctx", "exp"), P("ctx", "exp")),
        check_vma=False,
    )
```

time: 220 us -> 197 us (0.90)
  the two profiles are of different devices: /device:TPU:1 before, /device:TPU:32 now
where the time goes in v2:
time: 197 us; the launch traced here: 196 us
  blocking collectives  146 us (74%)
  starting transfers between devices  18.8 us (10%)
  Pallas kernels  15.8 us (8%)
  waiting for transfers between devices  9.75 us (5%)
  other arithmetic  2.58 us (1%)
  local copies, waits for them, and re-layouts  2.26 us (1%)
    all_gather x1, blocking collectives, per_device(): first = lax.all_gather(sent, 'ctx', axis=0)  39.2 us
    all_gather x1, blocking collectives, per_device(): second = lax.all_gather(rest, 'ctx', axis=0)  34.9 us
    all_gather x1, blocking collectives, per_device(): rows_all = lax.all_gather(normed, 'ctx', axis=0)  31 us
    all_to_all x1, blocking collectives, per_device(): pieces = lax.all_to_all(weigh(parts, combine), 'ctx', 0, 0)  26.2 us
    all_to_all x1, blocking collectives, per_device(): mine = lax.all_to_all(picked.reshape(exp_count, rows_dev, -1), 'exp', 0, 0)  15.1 us
    all_to_all x1, waiting for transfers between devices, per_device(): parts = lax.all_to_all(out, 'exp', 0, 0)  9.74 us
    pallas_call x1, Pallas kernels, run_experts(): pl.pallas_call(experts_kernel, out_shape=jax.ShapeDtypeStruct((D // 128,...  7.35 us
    all_to_all x1, starting transfers between devices, per_device(): heads = lax.all_to_all(spread, 'exp', 0, 0)  7.14 us
  transfers between devices with their start and end apart: 5, of which 1 were waited for; matrix products, arithmetic and copies ran while one was open for 2% of the time, Pallas kernels for 1%

profile of v2, /device:TPU:32, one launch (start us, length us, event | category | flops | bytes accessed | tf_op | source)
XLA Modules:
  0.0 196.5 jit_solution(17851733728774002229)
XLA Ops:
  0.6 0.0 copy-start.5
  0.7 0.0 copy-start.1
  0.7 0.0 copy-start.2
  0.7 0.0 copy-start.3
  0.7 3.8 %shard_map.122 = (bf16[12288,128]{1,0:T(8,128)(2,1)}, bf16[240,128]{1,0:T(8,128)(2,1)}) custom-call(s32[1]{0:T(128)} %bitcast.1.head_ref, bf16[4096,128]{1,0:T(8,128)(2,1)} %gate_ref.1, bf16[4096,128]{1,0:T(8,128)(2,1)} %up_ref.1, bf16[128,4096]{1,0:T(8,128)(2,1)} %down_ref.1, bf16[64,1024]{1,0:T(8,128)(2,1)} %key_ref.1, bf16[64,1024]{1,0:T(8,128)(2,1)} %value_ref.1, ...), custom_call_target="tpu_custom_call" | custom-call | tf_op jit(solution)/shard_map/pallas_call | solution.py:88
  4.5 0.0 copy-start.4
  4.5 3.4 %collective-permute-start = (bf16[12288,128]{1,0:T(8,128)(2,1)}, bf16[12288,128]{1,0:T(8,128)(2,1)}, u32[]{:S(2)}, u32[]{:S(2)}) collective-permute-start(bf16[12288,128]{1,0:T(8,128)(2,1)} %get-tuple-element.14.near_ref), channel_id=1, source_target_pairs={{0,2},{1,3},{2,0},{3,1},{4,6},{5,7},{6,4},{7,5},{8,10},{9,11},{10,... | collective-permute-start | bytes 9437192 | tf_op jit(solution)/shard_map/ppermute | solution.py:278
  7.9 0.0 copy-done.5
  8.0 0.1 convert_element_type.67
  8.0 39.2 %all-gather = bf16[3840,128]{1,0:T(8,128)(2,1)S(1)} all-gather(bf16[240,128]{1,0:T(8,128)(2,1)} %get-tuple-element.11), channel_id=2, replica_groups=mesh['ctx'=16,'exp'=32] {'ctx'}, dimensions={0}, use_global_device_ids=true | all-gather | bytes 1044480 | tf_op jit(solution)/shard_map/all_gather | solution.py:280
  47.2 0.0 copy-start
  47.2 0.0 copy-done.1
  47.2 0.0 copy-done.2
  47.2 0.0 copy-done.3
  47.2 1.4 shard_map.123
  48.6 7.1 %all-to-all-start = ((bf16[32,80,128]{2,1,0:T(8,128)(2,1)}), bf16[32,80,128]{2,1,0:T(8,128)(2,1)}, u32[]{:S(2)}, u32[]{:S(2)}) async-start(bf16[32,80,128]{2,1,0:T(8,128)(2,1)} %get-tuple-element.12), calls=%async_computation | async-start | bytes 1310720 | tf_op jit(solution)/shard_map/all_to_all | solution.py:290
  55.8 0.0 copy-done.4
  55.8 0.1 reshape.140
  55.9 0.1 convolution_bitcast_fusion
  56.1 0.1 select_reduce_fusion
  56.2 0.1 fusion.10
  56.3 0.1 convert_reduce_fusion.1
  56.4 0.7 copy.38.chosen_ref
  57.1 34.9 %all-gather.1 = bf16[2560,128]{1,0:T(8,128)(2,1)} all-gather(bf16[160,128]{1,0:T(8,128)(2,1)S(1)} %get-tuple-element.13), channel_id=3, replica_groups=mesh['ctx'=16,'exp'=32] {'ctx'}, dimensions={0}, use_global_device_ids=true | all-gather | bytes 696320 | tf_op jit(solution)/shard_map/all_gather | solution.py:291
  92.0 0.0 all-to-all-done.heads_ref
  92.0 0.0 collective-permute-done.far_ref
  92.0 0.0 copy-done
  92.0 2.8 %shard_map.124 = (bf16[64,128]{1,0:T(8,128)(2,1)}, bf16[128,128]{1,0:T(8,128)(2,1)}, f32[1,4096]{1,0:T(1,128)}, bf16[12288,128]{1,0:T(8,128)(2,1)}, bf16[12288,128]{1,0:T(8,128)(2,1)}) custom-call(bf16[32,80,128]{2,1,0:T(8,128)(2,1)} %all-to-all-done.heads_ref, bf16[16,240,128]{2,1,0:T(8,128)(2,1)} %bitcast.31, ...), custom_call_target="tpu_custom_call", output_to_operand_aliasing={{3}: (5, {}), {4}: (6, {})} | custom-call | tf_op jit(solution)/shard_map/pallas_call | solution.py:170
  94.7 1.9 collective-permute-start.1
  96.7 2.4 %collective-permute-start.2 = (bf16[12288,128]{1,0:T(8,128)(2,1)}, bf16[12288,128]{1,0:T(8,128)(2,1)}, u32[]{:S(2)}, u32[]{:S(2)}) collective-permute-start(bf16[12288,128]{1,0:T(8,128)(2,1)} %get-tuple-element.19.refs_2_), channel_id=1, source_target_pairs={{0,1},{1,0},{2,3},{3,2},{4,5},{5,4},{6,7},{7,6},{8,9},{9,8},{10,11... | collective-permute-start | bytes 9437192 | tf_op jit(solution)/shard_map/ppermute | solution.py:310
  99.1 15.1 %all_to_all.20 = bf16[32,4,128]{2,1,0:T(4,128)(2,1)S(1)} all-to-all(bf16[32,4,128]{2,1,0:T(4,128)(2,1)} %bitcast.35), channel_id=1, replica_groups=mesh['ctx'=16,'exp'=32] {'exp'}, dimensions={0} | all-to-all | bytes 65536 | tf_op jit(solution)/shard_map/all_to_all | solution.py:312
  114.1 0.1 fusion.6
  114.3 0.8 fusion.5
  115.1 31.0 %all_gather.20.x_ref = bf16[16,4,4096]{2,1,0:T(4,128)(2,1)} all-gather(bf16[1,4,4096]{2,1,0:T(4,128)(2,1)S(1)} %fusion.5), channel_id=1, replica_groups=mesh['ctx'=16,'exp'=32] {'ctx'}, dimensions={0}, use_global_device_ids=true | all-gather | bytes 557056 | tf_op jit(solution)/shard_map/all_gather | solution.py:316
  146.1 0.0 collective-permute-done.1.refs_1_
  146.1 0.0 collective-permute-done.2.refs_3_
  146.1 7.4 %shard_map.125 = bf16[32,64,128]{2,1,0:T(8,128)(2,1)} custom-call(bf16[16,4,4096]{2,1,0:T(4,128)(2,1)} %all_gather.20.x_ref, bf16[12288,128]{1,0:T(8,128)(2,1)} %get-tuple-element.18.refs_0_, bf16[12288,128]{1,0:T(8,128)(2,1)} %collective-permute-done.1.refs_1_, bf16[12288,128]{1,0:T(8,128)(2,1)} %get-tuple-element.19.refs_2_, ...), custom_call_target="tpu_custom_call" | custom-call | flops 805306368 | bytes 12582912 | tf_op jit(solution)/shard_map/pallas_call | solution.py:231
  153.5 3.9 %all-to-all-start.2 = ((bf16[32,64,128]{2,1,0:T(8,128)(2,1)}), bf16[32,64,128]{2,1,0:T(8,128)(2,1)S(1)}, u32[]{:S(2)}, u32[]{:S(2)}) async-start(bf16[32,64,128]{2,1,0:T(8,128)(2,1)} %shard_map.125), calls=%async_computation.2 | async-start | bytes 1048576 | tf_op jit(solution)/shard_map/all_to_all | solution.py:320
  157.4 0.8 slice_reduce_fusion.3
  158.2 0.1 reshape_squeeze.3
  158.3 0.1 slice_reduce_fusion.2
  158.3 0.1 broadcast_in_dim.33
  158.4 0.1 broadcast_in_dim.36
  158.6 0.1 eq.68
  158.6 0.1 eq.72
  158.7 0.7 fusion.2.combine_ref
  159.4 9.7 %all-to-all-done.2.parts_ref = bf16[32,64,128]{2,1,0:T(8,128)(2,1)S(1)} async-done(((bf16[32,64,128]{2,1,0:T(8,128)(2,1)}), bf16[32,64,128]{2,1,0:T(8,128)(2,1)S(1)}, u32[]{:S(2)}, u32[]{:S(2)}) %all-to-all-start.2) | async-done | bytes 524320 | tf_op jit(solution)/shard_map/all_to_all | solution.py:320
  169.2 0.4 shard_map.126
  169.6 26.2 %all_to_all.21 = bf16[16,64,128]{2,1,0:T(8,128)(2,1)S(1)} all-to-all(bf16[16,64,128]{2,1,0:T(8,128)(2,1)S(1)} %shard_map.126), channel_id=1, replica_groups=mesh['ctx'=16,'exp'=32] {'ctx'}, dimensions={0} | all-to-all | bytes 524288 | tf_op jit(solution)/shard_map/all_to_all | solution.py:321
  195.8 0.6 reduce_sum.52
  (9 shorter events, 0.2 us)
Async XLA Ops:
  0.6 7.3 %copy-start.5 = (f32[64,2]{0,1:T(2,128)S(1)}, f32[64,2]{0,1:T(2,128)}, u32[]{:S(2)}) copy-start(f32[64,2]{0,1:T(2,128)} %param.18) | copy-start | bytes 1540
  0.7 46.6 %copy-start.1 = (bf16[256,128]{1,0:T(8,128)(2,1)S(1)}, bf16[256,128]{1,0:T(8,128)(2,1)}, u32[]{:S(2)}) copy-start(bf16[256,128]{1,0:T(8,128)(2,1)} %proj_ref.3) | copy-start | bytes 196612
  0.7 46.6 %copy-start.2 = (bf16[64,128]{1,0:T(8,128)(2,1)S(1)}, bf16[64,128]{1,0:T(8,128)(2,1)}, u32[]{:S(2)}) copy-start(bf16[64,128]{1,0:T(8,128)(2,1)} %query_ref.1) | copy-start | bytes 49156
  0.7 46.6 %copy-start.3 = (f32[128]{0:T(128)S(1)}, f32[128]{0:T(128)}, u32[]{:S(2)}) copy-start(f32[128]{0:T(128)} %param.16) | copy-start | bytes 1540
  4.5 51.3 %copy-start.4 = (s32[1024,2]{0,1:T(2,128)S(1)}, s32[1024,2]{0,1:T(2,128)}, u32[]{:S(2)}) copy-start(s32[1024,2]{0,1:T(2,128)} %param.17) | copy-start | bytes 24580
  4.5 87.4 %collective-permute-start = (bf16[12288,128]{1,0:T(8,128)(2,1)}, bf16[12288,128]{1,0:T(8,128)(2,1)}, u32[]{:S(2)}, u32[]{:S(2)}) collective-permute-start(bf16[12288,128]{1,0:T(8,128)(2,1)} %get-tuple-element.14.near_ref), channel_id=1, source_target_pairs={{0,2},{1,3},{2,0},{3,1},{4,6},{5,7},{6,4},{7,5},{8,10},{9,11},{10,... | collective-permute-start | bytes 9437192 | tf_op jit(solution)/shard_map/ppermute | solution.py:278
  47.2 44.7 %copy-start = (bf16[3840,128]{1,0:T(8,128)(2,1)}, bf16[3840,128]{1,0:T(8,128)(2,1)S(1)}, u32[]{:S(2)}) copy-start(bf16[3840,128]{1,0:T(8,128)(2,1)S(1)} %all-gather) | copy-start | bytes 2949124
  48.6 43.3 %all-to-all-start = ((bf16[32,80,128]{2,1,0:T(8,128)(2,1)}), bf16[32,80,128]{2,1,0:T(8,128)(2,1)}, u32[]{:S(2)}, u32[]{:S(2)}) async-start(bf16[32,80,128]{2,1,0:T(8,128)(2,1)} %get-tuple-element.12), calls=%async_computation | async-start | bytes 1310720 | tf_op jit(solution)/shard_map/all_to_all | solution.py:290
  94.7 51.4 %collective-permute-start.1 = (bf16[12288,128]{1,0:T(8,128)(2,1)}, bf16[12288,128]{1,0:T(8,128)(2,1)}, u32[]{:S(2)}, u32[]{:S(2)}) collective-permute-start(bf16[12288,128]{1,0:T(8,128)(2,1)} %get-tuple-element.18.refs_0_), channel_id=1, source_target_pairs={{0,1},{1,0},{2,3},{3,2},{4,5},{5,4},{6,7},{7,6},{8,9},{9,8},{10,11... | collective-permute-start | bytes 9437192 | tf_op jit(solution)/shard_map/ppermute | solution.py:309
  96.7 49.5 %collective-permute-start.2 = (bf16[12288,128]{1,0:T(8,128)(2,1)}, bf16[12288,128]{1,0:T(8,128)(2,1)}, u32[]{:S(2)}, u32[]{:S(2)}) collective-permute-start(bf16[12288,128]{1,0:T(8,128)(2,1)} %get-tuple-element.19.refs_2_), channel_id=1, source_target_pairs={{0,1},{1,0},{2,3},{3,2},{4,5},{5,4},{6,7},{7,6},{8,9},{9,8},{10,11... | collective-permute-start | bytes 9437192 | tf_op jit(solution)/shard_map/ppermute | solution.py:310
  153.5 15.7 %all-to-all-start.2 = ((bf16[32,64,128]{2,1,0:T(8,128)(2,1)}), bf16[32,64,128]{2,1,0:T(8,128)(2,1)S(1)}, u32[]{:S(2)}, u32[]{:S(2)}) async-start(bf16[32,64,128]{2,1,0:T(8,128)(2,1)} %shard_map.125), calls=%async_computation.2 | async-start | bytes 1048576 | tf_op jit(solution)/shard_map/all_to_all | solution.py:320

commit v3 on v2

--- a/solution.py
+++ b/solution.py
@@ -22,6 +22,7 @@
 VMEM = pl.BlockSpec(memory_space=pltpu.VMEM)
 SMEM = pl.BlockSpec(memory_space=pltpu.SMEM)
 ANY = pl.BlockSpec(memory_space=pl.ANY)
+PACK_ROOM = 60 * 1024 * 1024
 ATTENTION_ROOM = 16 * 1024 * 1024
 ROOM = 63 * 1024 * 1024 - 512 * 1024
 F32 = jnp.float32
@@ -50,7 +51,7 @@
 
 def pack_kernel(
     head_ref, gate_ref, up_ref, down_ref, key_ref, value_ref, proj_ref,
-    out_ref, first_ref, gate_v, up_v, down_v, packed_v, sems,
+    out_ref, first_ref, down_v, sems,
 ):
     column = pl.ds(pl.multiple_of(head_ref[0] * HEAD_SIZE, HEAD_SIZE), HEAD_SIZE)
     copies = [
@@ -58,8 +59,8 @@
         for i, (src, dst) in enumerate(
             (
                 (down_ref, down_v),
-                (gate_ref, gate_v),
-                (up_ref, up_v),
+                (gate_ref, out_ref.at[pl.ds(0, D)]),
+                (up_ref, out_ref.at[pl.ds(D, D)]),
                 (key_ref.at[:, column], first_ref.at[pl.ds(0, SEG)]),
                 (value_ref.at[:, column], first_ref.at[pl.ds(SEG, SEG)]),
                 (proj_ref.at[pl.ds(0, W_FIRST)], first_ref.at[pl.ds(2 * SEG, W_FIRST)]),
@@ -68,19 +69,10 @@
     ]
     for copy in copies:
         copy.start()
-    outs = [
-        pltpu.make_async_copy(src, out_ref.at[pl.ds(i * D, D)], sems.at[6 + i])
-        for i, src in enumerate((gate_v, up_v, packed_v))
-    ]
     copies[0].wait()
     for b in range(D // 128):
-        packed_v[b * 128 : (b + 1) * 128] = down_v[:, b * 128 : (b + 1) * 128]
-    outs[2].start()
-    copies[1].wait()
-    outs[0].start()
-    copies[2].wait()
-    outs[1].start()
-    for copy in copies[3:] + outs:
+        out_ref[2 * D + b * 128 : 2 * D + (b + 1) * 128] = down_v[:, b * 128 : (b + 1) * 128]
+    for copy in copies[1:]:
         copy.wait()
 
 
@@ -92,15 +84,9 @@
             jax.ShapeDtypeStruct((2 * SEG + W_FIRST, HEAD_SIZE), BF16),
         ],
         in_specs=[SMEM] + [ANY] * 6,
-        out_specs=[ANY, VMEM],
-        scratch_shapes=[
-            pltpu.VMEM((D, 128), BF16),
-            pltpu.VMEM((D, 128), BF16),
-            pltpu.VMEM((128, D), BF16),
-            pltpu.VMEM((D, 128), BF16),
-            pltpu.SemaphoreType.DMA((9,)),
-        ],
-        compiler_params=pltpu.CompilerParams(vmem_limit_bytes=ROOM),
+        out_specs=[VMEM, VMEM],
+        scratch_shapes=[pltpu.VMEM((128, D), BF16), pltpu.SemaphoreType.DMA((6,))],
+        compiler_params=pltpu.CompilerParams(vmem_limit_bytes=PACK_ROOM),
     )(head, w_gate, w_up, w_down, keys, values, out_proj)
 
 
@@ -108,7 +94,11 @@
     ctx_ref, query_ref, first_ref, gain_ref, gate_ref, proj_ref, out_ref, second_ref
 ):
     second_ref[: proj_ref.shape[0] - W_FIRST] = proj_ref[W_FIRST:]
-    second_ref[proj_ref.shape[0] - W_FIRST :] = gate_ref[...]
+    wts = jnp.concatenate([gate_ref[...], jnp.zeros((TOP, HEAD_SIZE - SEG), F32)], axis=1)
+    line = lax.broadcasted_iota(jnp.int32, (EXTRA, HEAD_SIZE), 0)
+    second_ref[proj_ref.shape[0] - W_FIRST :] = jnp.where(
+        line == 0, wts[0:1], jnp.where(line == 1, wts[1:2], 0.0)
+    ).astype(BF16)
     count = SHARDS * SEG
     key_all = first_ref[:, :SEG].reshape(count, HEAD_SIZE)
     value_all = first_ref[:, SEG : 2 * SEG].reshape(count, HEAD_SIZE)
@@ -122,7 +112,6 @@
     total = jnp.sum(weights, axis=1, keepdims=True)
     attn = jnp.dot(weights.astype(BF16), value_all, preferred_element_type=F32)
     gains = three_terms(jnp.broadcast_to(gain_ref[...], (EXTRA, HEAD_SIZE)))
-    line = lax.broadcasted_iota(jnp.int32, (EXTRA, HEAD_SIZE), 0)
     gain_rows = jnp.zeros((EXTRA, HEAD_SIZE), F32)
     for k in range(3):
         gain_rows = jnp.where(line == k, gains[k].astype(F32), gain_rows)
@@ -130,7 +119,7 @@
     out_ref[...] = jnp.broadcast_to(sent[None], out_ref.shape)
 
 
-def attention(ctx_rank, queries, first, gain, gate_rows, out_proj):
+def attention(ctx_rank, queries, first, gain, wts, out_proj):
     return pl.pallas_call(
         attention_kernel,
         out_shape=[
@@ -140,14 +129,13 @@
         in_specs=[SMEM] + [VMEM] * 5,
         out_specs=[VMEM, VMEM],
         compiler_params=pltpu.CompilerParams(vmem_limit_bytes=ATTENTION_ROOM),
-    )(ctx_rank, queries, first, gain, gate_rows, out_proj)
+    )(ctx_rank, queries, first, gain, wts, out_proj)
 
 
 def project_kernel(
-    heads_ref, first_ref, second_ref, residual_ref, chosen_ref, near_ref, far_ref,
-    out_ref, picked_ref, gain_ref, near_out, far_out, attn_v, proj_v,
+    ctx_ref, heads_ref, first_ref, second_ref, residual_ref, place_ref,
+    out_ref, picked_ref, gain_ref, attn_v, proj_v,
 ):
-    del near_ref, far_ref, near_out, far_out
     for h in range(QUERY_HEAD_COUNT):
         attn_v[:, h * 128 : (h + 1) * 128] = heads_ref[h, :SEG]
         gain_ref[:, h * 128 : (h + 1) * 128] = jnp.sum(
@@ -161,27 +149,40 @@
     )
     rounded = residual.astype(BF16)
     out_ref[...] = rounded
-    picked_ref[...] = jnp.dot(
-        chosen_ref[...], rounded, preferred_element_type=F32
-    ).astype(BF16)
-
-
-def project(heads, first, second, residual_in, chosen, near, far):
+    line = lax.broadcasted_iota(jnp.int32, (EXPERTS * CAP, SEG), 0)
+    place = place_ref[ctx_ref[0]]
+    chosen = jnp.where((line == place[0:1]) | (line == place[1:2]), 1.0, 0.0)
+    picked_ref[...] = jnp.dot(chosen.astype(BF16), rounded, preferred_element_type=F32).astype(BF16)
+
+
+def project(ctx_rank, heads, first, second, residual_in, place):
     return pl.pallas_call(
         project_kernel,
         out_shape=[
             jax.ShapeDtypeStruct((SEG, 128), BF16),
             jax.ShapeDtypeStruct((EXPERTS * CAP, 128), BF16),
             jax.ShapeDtypeStruct((1, D), F32),
-            jax.ShapeDtypeStruct(near.shape, near.dtype),
-            jax.ShapeDtypeStruct(far.shape, far.dtype),
         ],
-        in_specs=[VMEM] * 5 + [ANY] * 2,
-        out_specs=[VMEM] * 3 + [ANY] * 2,
+        in_specs=[SMEM] + [VMEM] * 5,
+        out_specs=[VMEM] * 3,
         scratch_shapes=[pltpu.VMEM((SEG, D), BF16), pltpu.VMEM((D, 128), BF16)],
-        input_output_aliases={5: 3, 6: 4},
+        compiler_params=pltpu.CompilerParams(vmem_limit_bytes=ATTENTION_ROOM),
+    )(ctx_rank, heads, first, second, residual_in, place)
+
+
+def after_kernel(near_ref, far_ref, other_ref, near_out, far_out):
+    del near_ref, far_ref, other_ref, near_out, far_out
+
+
+def after(near, far, other):
+    return pl.pallas_call(
+        after_kernel,
+        out_shape=[jax.ShapeDtypeStruct(v.shape, v.dtype) for v in (near, far)],
+        in_specs=[ANY, ANY, ANY],
+        out_specs=[ANY, ANY],
+        input_output_aliases={0: 0, 1: 1},
         compiler_params=pltpu.CompilerParams(vmem_limit_bytes=ROOM),
-    )(heads, first, second, residual_in, chosen, near, far)
+    )(near, far, other)
 
 
 def experts_kernel(x_ref, *refs):
@@ -195,7 +196,7 @@
             )
     for copy in copies:
         copy.start()
-    x = jnp.concatenate([x_ref[c].astype(F32) for c in range(SHARDS)], axis=0).astype(BF16)
+    x = x_ref[...]
     for i in range(4):
         copies[i].wait()
         both = jnp.dot(
@@ -227,7 +228,7 @@
 
 
 def run_experts(rows_all, weights):
-    rows = rows_all.shape[0] * rows_all.shape[1]
+    rows = rows_all.shape[0]
     return pl.pallas_call(
         experts_kernel,
         out_shape=jax.ShapeDtypeStruct((D // 128, rows, 128), BF16),
@@ -273,28 +274,26 @@
     pair = [(i, i ^ 1) for i in range(exp_count)]
     chip = [(i, i ^ 2) for i in range(exp_count)]
 
+    ctx = ctx_rank.astype(jnp.int32).reshape(1)
+
     head = (exp_rank // (QUERY_HEAD_COUNT // KEY_VALUE_HEADS)).astype(jnp.int32).reshape(1)
     near, sent = pack(head, w_gate, w_up, w_down, keys, values, out_proj)
     far = lax.ppermute(near, "exp", chip)
 
     first = lax.all_gather(sent, "ctx", axis=0)
-    gate_row = gate_wts.T.reshape(1, TOP * SEG).astype(BF16)
     spread, rest = attention(
-        ctx_rank.astype(jnp.int32).reshape(1),
+        ctx,
         queries,
         first,
         norm_gain.reshape(1, -1),
-        jnp.concatenate([gate_row, jnp.zeros((EXTRA - 1, TOP * SEG), BF16)], axis=0),
+        gate_wts.T,
         out_proj,
     )
     heads = lax.all_to_all(spread, "exp", 0, 0)
     second = lax.all_gather(rest, "ctx", axis=0)
-    gate_all = second[:, -EXTRA].reshape(ctx_count, TOP, SEG)
+    gate_all = second[:, -EXTRA : TOP - EXTRA, :SEG]
 
     place = slot_places(routes.reshape(ctx_count, SEG, TOP))
-    own_place = lax.dynamic_index_in_dim(place, ctx_rank, 0, keepdims=False)
-    slot_ids = jnp.arange(EXPERTS * CAP, dtype=jnp.int32)
-    chosen = (own_place.T[:, None, :] == slot_ids[None, :, None]).astype(F32).sum(axis=0)
     shard = jnp.arange(ctx_count, dtype=jnp.int32)[:, None, None] % 4
     column = (place // rows_dev) * 16 + shard * rows_dev + place % rows_dev
     columns = jnp.arange(exp_count * 16, dtype=jnp.int32)
@@ -303,9 +302,10 @@
         for k in range(TOP)
     ).reshape(ctx_count // 4, 4 * SEG, exp_count * 16)
 
-    residual_out, picked, gain_all, near, far = project(
-        heads, first, second, residual_in, chosen.astype(BF16), near, far
-    )
+    residual_out, picked, gain_all = project(
+        ctx, heads, first, second, residual_in, place.transpose(0, 2, 1)
+    )
+    near, far = after(near, far, residual_out)
     across = lax.ppermute(near, "exp", pair)
     across_far = lax.ppermute(far, "exp", pair)
 
@@ -313,7 +313,7 @@
     mine = mine.transpose(1, 0, 2).reshape(rows_dev, D).astype(F32)
     sq_mean = jnp.mean(mine * mine, axis=1, keepdims=True)
     normed = (mine * lax.rsqrt(sq_mean + 1e-05) * gain_all).astype(BF16)
-    rows_all = lax.all_gather(normed, "ctx", axis=0)
+    rows_all = lax.all_gather(normed, "ctx", axis=0).reshape(ctx_count * rows_dev, D)
 
     out = run_experts(rows_all, [near, across, far, across_far])
 

time: 197 us -> 193 us (0.980)
  Pallas kernels: 15.8 us -> 13.8 us
    all_gather x1, blocking collectives: 34.9 us -> 32.5 us  [per_device(): second = lax.all_gather(rest, 'ctx', axis=0)]
  transfers between devices with their start and end apart: 5 -> 5, of which waited for: 1 -> 1; matrix products, arithmetic and copies ran while one was open for 2% -> 1% of each run, Pallas kernels for 1% -> 1%
where the time goes in v3:
time: 193 us; the launch traced here: 192 us
  blocking collectives  145 us (75%)
  starting transfers between devices  18.6 us (10%)
  Pallas kernels  13.8 us (7%)
  waiting for transfers between devices  10.6 us (5%)
    all_gather x1, blocking collectives, per_device(): first = lax.all_gather(sent, 'ctx', axis=0)  39.2 us
    all_gather x1, blocking collectives, per_device(): second = lax.all_gather(rest, 'ctx', axis=0)  32.5 us
    all_gather x1, blocking collectives, per_device(): lax.all_gather(normed, 'ctx', axis=0).reshape(ctx_count * rows_dev, D)  31 us
    all_to_all x1, blocking collectives, per_device(): pieces = lax.all_to_all(weigh(parts, combine), 'ctx', 0, 0)  27.3 us
    all_to_all x1, blocking collectives, per_device(): mine = lax.all_to_all(picked.reshape(exp_count, rows_dev, -1), 'exp', 0, 0)  14.7 us
    all_to_all x1, waiting for transfers between devices, per_device(): parts = lax.all_to_all(out, 'exp', 0, 0)  10.6 us
    pallas_call x1, Pallas kernels, run_experts(): pl.pallas_call(experts_kernel, out_shape=jax.ShapeDtypeStruct((D // 128,...  7.38 us
    all_to_all x1, starting transfers between devices, per_device(): heads = lax.all_to_all(spread, 'exp', 0, 0)  7.03 us
  transfers between devices with their start and end apart: 5, of which 1 were waited for; matrix products, arithmetic and copies ran while one was open for 1% of the time, Pallas kernels for 1%

profile of v3, /device:TPU:32, one launch (start us, length us, event | category | flops | bytes accessed | tf_op | source)
XLA Modules:
  0.0 192.1 jit_solution(9172849659655310262)
XLA Ops:
  0.6 0.0 copy-start
  0.7 0.0 copy-start.1
  0.7 0.0 copy-start.3
  0.7 0.0 copy-start.4
  0.7 3.6 %shard_map.122 = (bf16[12288,128]{1,0:T(8,128)(2,1)}, bf16[240,128]{1,0:T(8,128)(2,1)}) custom-call(s32[1]{0:T(128)} %bitcast.1.head_ref, bf16[4096,128]{1,0:T(8,128)(2,1)} %gate_ref.1, bf16[4096,128]{1,0:T(8,128)(2,1)} %up_ref.1, bf16[128,4096]{1,0:T(8,128)(2,1)} %down_ref.1, bf16[64,1024]{1,0:T(8,128)(2,1)} %key_ref.1, bf16[64,1024]{1,0:T(8,128)(2,1)} %value_ref.1, ...), custom_call_target="tpu_custom_call" | custom-call | tf_op jit(solution)/shard_map/pallas_call | solution.py:80
  4.3 0.0 copy-start.5
  4.3 3.4 %collective-permute-start = (bf16[12288,128]{1,0:T(8,128)(2,1)}, bf16[12288,128]{1,0:T(8,128)(2,1)}, u32[]{:S(2)}, u32[]{:S(2)}) collective-permute-start(bf16[12288,128]{1,0:T(8,128)(2,1)} %get-tuple-element.17.near_ref), channel_id=1, source_target_pairs={{0,2},{1,3},{2,0},{3,1},{4,6},{5,7},{6,4},{7,5},{8,10},{9,11},{10,... | collective-permute-start | bytes 9437192 | tf_op jit(solution)/shard_map/ppermute | solution.py:281
  7.8 0.0 copy-start.2
  7.8 39.2 %all-gather = bf16[3840,128]{1,0:T(8,128)(2,1)S(1)} all-gather(bf16[240,128]{1,0:T(8,128)(2,1)} %get-tuple-element.11), channel_id=2, replica_groups=mesh['ctx'=16,'exp'=32] {'ctx'}, dimensions={0}, use_global_device_ids=true | all-gather | bytes 1044480 | tf_op jit(solution)/shard_map/all_gather | solution.py:283
  47.0 0.0 copy-done
  47.0 0.0 copy-done.1
  47.0 0.0 copy-done.3
  47.0 0.0 copy-done.4
  47.0 1.4 shard_map.123
  48.3 7.0 %all-to-all-start = ((bf16[32,80,128]{2,1,0:T(8,128)(2,1)}), bf16[32,80,128]{2,1,0:T(8,128)(2,1)S(1)}, u32[]{:S(2)}, u32[]{:S(2)}) async-start(bf16[32,80,128]{2,1,0:T(8,128)(2,1)} %get-tuple-element.12), calls=%async_computation | async-start | bytes 1310720 | tf_op jit(solution)/shard_map/all_to_all | solution.py:292
  55.4 0.0 copy-done.5
  55.4 0.1 reshape.128
  55.5 0.1 convolution_bitcast_fusion
  55.7 0.1 select_reduce_fusion
  55.8 0.1 fusion.10
  55.8 32.5 %all-gather.1 = bf16[2560,128]{1,0:T(8,128)(2,1)S(1)} all-gather(bf16[160,128]{1,0:T(8,128)(2,1)S(1)} %get-tuple-element.13), channel_id=3, replica_groups=mesh['ctx'=16,'exp'=32] {'ctx'}, dimensions={0}, use_global_device_ids=true | all-gather | bytes 696320 | tf_op jit(solution)/shard_map/all_gather | solution.py:293
  88.4 0.0 all-to-all-done.heads_ref
  88.4 0.0 copy-done.2
  88.4 1.0 shard_map.124
  89.4 0.0 collective-permute-done.far_ref
  89.4 1.9 collective-permute-start.1
  91.3 2.4 %collective-permute-start.2 = (bf16[12288,128]{1,0:T(8,128)(2,1)}, bf16[12288,128]{1,0:T(8,128)(2,1)}, u32[]{:S(2)}, u32[]{:S(2)}) collective-permute-start(bf16[12288,128]{1,0:T(8,128)(2,1)} %get-tuple-element.19.refs_2_), channel_id=1, source_target_pairs={{0,1},{1,0},{2,3},{3,2},{4,5},{5,4},{6,7},{7,6},{8,9},{9,8},{10,11... | collective-permute-start | bytes 9437192 | tf_op jit(solution)/shard_map/ppermute | solution.py:310
  93.8 14.7 %all_to_all.20 = bf16[32,4,128]{2,1,0:T(4,128)(2,1)S(1)} all-to-all(bf16[32,4,128]{2,1,0:T(4,128)(2,1)S(1)} %bitcast.31), channel_id=1, replica_groups=mesh['ctx'=16,'exp'=32] {'exp'}, dimensions={0} | all-to-all | bytes 65536 | tf_op jit(solution)/shard_map/all_to_all | solution.py:312
  108.4 0.1 fusion.6
  108.6 0.1 fusion.5
  108.7 31.0 %all_gather.20 = bf16[16,4,4096]{2,1,0:T(4,128)(2,1)S(1)} all-gather(bf16[1,4,4096]{2,1,0:T(4,128)(2,1)S(1)} %fusion.5), channel_id=1, replica_groups=mesh['ctx'=16,'exp'=32] {'ctx'}, dimensions={0}, use_global_device_ids=true | all-gather | bytes 557056 | tf_op jit(solution)/shard_map/all_gather | solution.py:316
  139.7 0.9 reshape.130.x_ref
  140.7 0.0 collective-permute-done.1.refs_1_
  140.7 0.0 collective-permute-done.2.refs_3_
  140.7 7.4 %shard_map.126 = bf16[32,64,128]{2,1,0:T(8,128)(2,1)} custom-call(bf16[64,4096]{1,0:T(8,128)(2,1)} %reshape.130.x_ref, bf16[12288,128]{1,0:T(8,128)(2,1)} %get-tuple-element.18.refs_0_, bf16[12288,128]{1,0:T(8,128)(2,1)} %collective-permute-done.1.refs_1_, bf16[12288,128]{1,0:T(8,128)(2,1)} %get-tuple-element.19.refs_2_, ...), custom_call_target="tpu_custom_call" | custom-call | flops 805306368 | bytes 12582912 | tf_op jit(solution)/shard_map/pallas_call | solution.py:232
  148.1 3.9 %all-to-all-start.2 = ((bf16[32,64,128]{2,1,0:T(8,128)(2,1)}), bf16[32,64,128]{2,1,0:T(8,128)(2,1)S(1)}, u32[]{:S(2)}, u32[]{:S(2)}) async-start(bf16[32,64,128]{2,1,0:T(8,128)(2,1)} %shard_map.126), calls=%async_computation.2 | async-start | bytes 1048576 | tf_op jit(solution)/shard_map/all_to_all | solution.py:320
  152.0 0.1 slice_reduce_fusion.2
  152.0 0.1 broadcast_in_dim.30
  152.1 0.1 broadcast_in_dim.33
  152.2 0.1 eq.52
  152.3 0.1 eq.56
  152.4 0.7 fusion.2.combine_ref
  153.1 10.6 %all-to-all-done.2.parts_ref = bf16[32,64,128]{2,1,0:T(8,128)(2,1)S(1)} async-done(((bf16[32,64,128]{2,1,0:T(8,128)(2,1)}), bf16[32,64,128]{2,1,0:T(8,128)(2,1)S(1)}, u32[]{:S(2)}, u32[]{:S(2)}) %all-to-all-start.2) | async-done | bytes 524320 | tf_op jit(solution)/shard_map/all_to_all | solution.py:320
  163.7 0.4 shard_map.127
  164.1 27.3 %all_to_all.21 = bf16[16,64,128]{2,1,0:T(8,128)(2,1)S(1)} all-to-all(bf16[16,64,128]{2,1,0:T(8,128)(2,1)S(1)} %shard_map.127), channel_id=1, replica_groups=mesh['ctx'=16,'exp'=32] {'ctx'}, dimensions={0} | all-to-all | bytes 524288 | tf_op jit(solution)/shard_map/all_to_all | solution.py:321
  191.4 0.6 reduce_sum.42
  (7 shorter events, 0.1 us)
Async XLA Ops:
  0.6 46.3 %copy-start = (bf16[256,128]{1,0:T(8,128)(2,1)S(1)}, bf16[256,128]{1,0:T(8,128)(2,1)}, u32[]{:S(2)}) copy-start(bf16[256,128]{1,0:T(8,128)(2,1)} %proj_ref.3) | copy-start | bytes 196612
  0.7 46.3 %copy-start.1 = (bf16[64,128]{1,0:T(8,128)(2,1)S(1)}, bf16[64,128]{1,0:T(8,128)(2,1)}, u32[]{:S(2)}) copy-start(bf16[64,128]{1,0:T(8,128)(2,1)} %query_ref.1) | copy-start | bytes 49156
  0.7 46.3 %copy-start.3 = (f32[64,2]{0,1:T(2,128)S(1)}, f32[64,2]{0,1:T(2,128)}, u32[]{:S(2)}) copy-start(f32[64,2]{0,1:T(2,128)} %param.18) | copy-start | bytes 1540
  0.7 46.3 %copy-start.4 = (f32[128]{0:T(128)S(1)}, f32[128]{0:T(128)}, u32[]{:S(2)}) copy-start(f32[128]{0:T(128)} %param.16) | copy-start | bytes 1540
  4.3 51.0 %copy-start.5 = (s32[1024,2]{0,1:T(2,128)S(1)}, s32[1024,2]{0,1:T(2,128)}, u32[]{:S(2)}) copy-start(s32[1024,2]{0,1:T(2,128)} %param.17) | copy-start | bytes 24580
  4.3 85.1 %collective-permute-start = (bf16[12288,128]{1,0:T(8,128)(2,1)}, bf16[12288,128]{1,0:T(8,128)(2,1)}, u32[]{:S(2)}, u32[]{:S(2)}) collective-permute-start(bf16[12288,128]{1,0:T(8,128)(2,1)} %get-tuple-element.17.near_ref), channel_id=1, source_target_pairs={{0,2},{1,3},{2,0},{3,1},{4,6},{5,7},{6,4},{7,5},{8,10},{9,11},{10,... | collective-permute-start | bytes 9437192 | tf_op jit(solution)/shard_map/ppermute | solution.py:281
  7.8 80.6 %copy-start.2 = (bf16[64,128]{1,0:T(8,128)(2,1)S(1)}, bf16[64,128]{1,0:T(8,128)(2,1)}, u32[]{:S(2)}) copy-start(bf16[64,128]{1,0:T(8,128)(2,1)} %residual_ref.1) | copy-start | bytes 49156
  48.3 40.0 %all-to-all-start = ((bf16[32,80,128]{2,1,0:T(8,128)(2,1)}), bf16[32,80,128]{2,1,0:T(8,128)(2,1)S(1)}, u32[]{:S(2)}, u32[]{:S(2)}) async-start(bf16[32,80,128]{2,1,0:T(8,128)(2,1)} %get-tuple-element.12), calls=%async_computation | async-start | bytes 1310720 | tf_op jit(solution)/shard_map/all_to_all | solution.py:292
  89.4 51.2 %collective-permute-start.1 = (bf16[12288,128]{1,0:T(8,128)(2,1)}, bf16[12288,128]{1,0:T(8,128)(2,1)}, u32[]{:S(2)}, u32[]{:S(2)}) collective-permute-start(bf16[12288,128]{1,0:T(8,128)(2,1)} %get-tuple-element.18.refs_0_), channel_id=1, source_target_pairs={{0,1},{1,0},{2,3},{3,2},{4,5},{5,4},{6,7},{7,6},{8,9},{9,8},{10,11... | collective-permute-start | bytes 9437192 | tf_op jit(solution)/shard_map/ppermute | solution.py:309
  91.3 49.3 %collective-permute-start.2 = (bf16[12288,128]{1,0:T(8,128)(2,1)}, bf16[12288,128]{1,0:T(8,128)(2,1)}, u32[]{:S(2)}, u32[]{:S(2)}) collective-permute-start(bf16[12288,128]{1,0:T(8,128)(2,1)} %get-tuple-element.19.refs_2_), channel_id=1, source_target_pairs={{0,1},{1,0},{2,3},{3,2},{4,5},{5,4},{6,7},{7,6},{8,9},{9,8},{10,11... | collective-permute-start | bytes 9437192 | tf_op jit(solution)/shard_map/ppermute | solution.py:310
  148.1 15.7 %all-to-all-start.2 = ((bf16[32,64,128]{2,1,0:T(8,128)(2,1)}), bf16[32,64,128]{2,1,0:T(8,128)(2,1)S(1)}, u32[]{:S(2)}, u32[]{:S(2)}) async-start(bf16[32,64,128]{2,1,0:T(8,128)(2,1)} %shard_map.126), calls=%async_computation.2 | async-start | bytes 1048576 | tf_op jit(solution)/shard_map/all_to_all | solution.py:320

commit v4 on v3

--- a/solution.py
+++ b/solution.py
@@ -16,7 +16,7 @@
 CAP = 16
 SEG = 64
 SHARDS = 16
-W_FIRST = 112
+W_FIRST = 64
 EXTRA = 16
 
 VMEM = pl.BlockSpec(memory_space=pltpu.VMEM)

time: 193 us -> 193 us (level)
  no operation moved by 1% of the time
where the time goes in v4:
time: 193 us; the launch traced here: 192 us
  blocking collectives  145 us (75%)
  starting transfers between devices  18.6 us (10%)
  Pallas kernels  13.8 us (7%)
  waiting for transfers between devices  10.6 us (5%)
    all_gather x1, blocking collectives, per_device(): first = lax.all_gather(sent, 'ctx', axis=0)  37.9 us
    all_gather x1, blocking collectives, per_device(): second = lax.all_gather(rest, 'ctx', axis=0)  33.9 us
    all_gather x1, blocking collectives, per_device(): lax.all_gather(normed, 'ctx', axis=0).reshape(ctx_count * rows_dev, D)  31.2 us
    all_to_all x1, blocking collectives, per_device(): pieces = lax.all_to_all(weigh(parts, combine), 'ctx', 0, 0)  27.3 us
    all_to_all x1, blocking collectives, per_device(): mine = lax.all_to_all(picked.reshape(exp_count, rows_dev, -1), 'exp', 0, 0)  14.4 us
    all_to_all x1, waiting for transfers between devices, per_device(): parts = lax.all_to_all(out, 'exp', 0, 0)  10.6 us
    pallas_call x1, Pallas kernels, run_experts(): pl.pallas_call(experts_kernel, out_shape=jax.ShapeDtypeStruct((D // 128,...  7.38 us
    all_to_all x1, starting transfers between devices, per_device(): heads = lax.all_to_all(spread, 'exp', 0, 0)  7.03 us
  transfers between devices with their start and end apart: 5, of which 1 were waited for; matrix products, arithmetic and copies ran while one was open for 1% of the time, Pallas kernels for 1%

profile of v4, /device:TPU:32, one launch (start us, length us, event | category | flops | bytes accessed | tf_op | source)
XLA Modules:
  0.0 192.1 jit_solution(8138843057135970083)
XLA Ops:
  0.6 0.0 copy-start
  0.7 0.0 copy-start.2
  0.7 0.0 copy-start.3
  0.7 0.0 copy-start.4
  0.7 3.6 %shard_map.122 = (bf16[12288,128]{1,0:T(8,128)(2,1)}, bf16[192,128]{1,0:T(8,128)(2,1)}) custom-call(s32[1]{0:T(128)} %bitcast.1.head_ref, bf16[4096,128]{1,0:T(8,128)(2,1)} %gate_ref.1, bf16[4096,128]{1,0:T(8,128)(2,1)} %up_ref.1, bf16[128,4096]{1,0:T(8,128)(2,1)} %down_ref.1, bf16[64,1024]{1,0:T(8,128)(2,1)} %key_ref.1, bf16[64,1024]{1,0:T(8,128)(2,1)} %value_ref.1, ...), custom_call_target="tpu_custom_call" | custom-call | tf_op jit(solution)/shard_map/pallas_call | solution.py:80
  4.3 0.0 copy-start.5
  4.3 3.4 %collective-permute-start = (bf16[12288,128]{1,0:T(8,128)(2,1)}, bf16[12288,128]{1,0:T(8,128)(2,1)}, u32[]{:S(2)}, u32[]{:S(2)}) collective-permute-start(bf16[12288,128]{1,0:T(8,128)(2,1)} %get-tuple-element.17.near_ref), channel_id=1, source_target_pairs={{0,2},{1,3},{2,0},{3,1},{4,6},{5,7},{6,4},{7,5},{8,10},{9,11},{10,... | collective-permute-start | bytes 9437192 | tf_op jit(solution)/shard_map/ppermute | solution.py:281
  7.7 0.0 copy-start.1
  7.8 37.9 %all-gather = bf16[3072,128]{1,0:T(8,128)(2,1)S(1)} all-gather(bf16[192,128]{1,0:T(8,128)(2,1)} %get-tuple-element.11), channel_id=2, replica_groups=mesh['ctx'=16,'exp'=32] {'ctx'}, dimensions={0}, use_global_device_ids=true | all-gather | bytes 835584 | tf_op jit(solution)/shard_map/all_gather | solution.py:283
  45.7 0.0 copy-done
  45.7 0.0 copy-done.2
  45.7 0.0 copy-done.3
  45.7 0.0 copy-done.4
  45.7 1.4 shard_map.123
  47.0 7.0 %all-to-all-start = ((bf16[32,80,128]{2,1,0:T(8,128)(2,1)}), bf16[32,80,128]{2,1,0:T(8,128)(2,1)S(1)}, u32[]{:S(2)}, u32[]{:S(2)}) async-start(bf16[32,80,128]{2,1,0:T(8,128)(2,1)} %get-tuple-element.12), calls=%async_computation | async-start | bytes 1310720 | tf_op jit(solution)/shard_map/all_to_all | solution.py:292
  54.1 0.0 copy-done.5
  54.1 0.1 reshape.128
  54.2 0.1 convolution_bitcast_fusion
  54.4 0.1 select_reduce_fusion
  54.5 0.1 fusion.10
  54.5 33.9 %all-gather.1 = bf16[3328,128]{1,0:T(8,128)(2,1)S(1)} all-gather(bf16[208,128]{1,0:T(8,128)(2,1)S(1)} %get-tuple-element.13), channel_id=3, replica_groups=mesh['ctx'=16,'exp'=32] {'ctx'}, dimensions={0}, use_global_device_ids=true | all-gather | bytes 905216 | tf_op jit(solution)/shard_map/all_gather | solution.py:293
  88.4 0.0 all-to-all-done.heads_ref
  88.4 0.0 copy-done.1
  88.4 1.0 shard_map.124
  89.5 0.0 collective-permute-done.far_ref
  89.5 1.9 collective-permute-start.1
  91.4 2.4 %collective-permute-start.2 = (bf16[12288,128]{1,0:T(8,128)(2,1)}, bf16[12288,128]{1,0:T(8,128)(2,1)}, u32[]{:S(2)}, u32[]{:S(2)}) collective-permute-start(bf16[12288,128]{1,0:T(8,128)(2,1)} %get-tuple-element.19.refs_2_), channel_id=1, source_target_pairs={{0,1},{1,0},{2,3},{3,2},{4,5},{5,4},{6,7},{7,6},{8,9},{9,8},{10,11... | collective-permute-start | bytes 9437192 | tf_op jit(solution)/shard_map/ppermute | solution.py:310
  93.8 14.4 %all_to_all.20 = bf16[32,4,128]{2,1,0:T(4,128)(2,1)S(1)} all-to-all(bf16[32,4,128]{2,1,0:T(4,128)(2,1)S(1)} %bitcast.31), channel_id=1, replica_groups=mesh['ctx'=16,'exp'=32] {'exp'}, dimensions={0} | all-to-all | bytes 65536 | tf_op jit(solution)/shard_map/all_to_all | solution.py:312
  108.2 0.1 fusion.6
  108.4 0.1 fusion.5
  108.5 31.2 %all_gather.20 = bf16[16,4,4096]{2,1,0:T(4,128)(2,1)S(1)} all-gather(bf16[1,4,4096]{2,1,0:T(4,128)(2,1)S(1)} %fusion.5), channel_id=1, replica_groups=mesh['ctx'=16,'exp'=32] {'ctx'}, dimensions={0}, use_global_device_ids=true | all-gather | bytes 557056 | tf_op jit(solution)/shard_map/all_gather | solution.py:316
  139.7 0.9 reshape.130.x_ref
  140.6 0.0 collective-permute-done.1.refs_1_
  140.6 0.0 collective-permute-done.2.refs_3_
  140.6 7.4 %shard_map.126 = bf16[32,64,128]{2,1,0:T(8,128)(2,1)} custom-call(bf16[64,4096]{1,0:T(8,128)(2,1)} %reshape.130.x_ref, bf16[12288,128]{1,0:T(8,128)(2,1)} %get-tuple-element.18.refs_0_, bf16[12288,128]{1,0:T(8,128)(2,1)} %collective-permute-done.1.refs_1_, bf16[12288,128]{1,0:T(8,128)(2,1)} %get-tuple-element.19.refs_2_, ...), custom_call_target="tpu_custom_call" | custom-call | flops 805306368 | bytes 12582912 | tf_op jit(solution)/shard_map/pallas_call | solution.py:232
  148.0 3.9 %all-to-all-start.2 = ((bf16[32,64,128]{2,1,0:T(8,128)(2,1)}), bf16[32,64,128]{2,1,0:T(8,128)(2,1)S(1)}, u32[]{:S(2)}, u32[]{:S(2)}) async-start(bf16[32,64,128]{2,1,0:T(8,128)(2,1)} %shard_map.126), calls=%async_computation.2 | async-start | bytes 1048576 | tf_op jit(solution)/shard_map/all_to_all | solution.py:320
  151.9 0.1 slice_reduce_fusion.2
  152.0 0.1 broadcast_in_dim.30
  152.1 0.1 broadcast_in_dim.33
  152.2 0.1 eq.52
  152.3 0.1 eq.56
  152.4 0.7 fusion.2.combine_ref
  153.1 10.6 %all-to-all-done.2.parts_ref = bf16[32,64,128]{2,1,0:T(8,128)(2,1)S(1)} async-done(((bf16[32,64,128]{2,1,0:T(8,128)(2,1)}), bf16[32,64,128]{2,1,0:T(8,128)(2,1)S(1)}, u32[]{:S(2)}, u32[]{:S(2)}) %all-to-all-start.2) | async-done | bytes 524320 | tf_op jit(solution)/shard_map/all_to_all | solution.py:320
  163.7 0.4 shard_map.127
  164.1 27.3 %all_to_all.21 = bf16[16,64,128]{2,1,0:T(8,128)(2,1)S(1)} all-to-all(bf16[16,64,128]{2,1,0:T(8,128)(2,1)S(1)} %shard_map.127), channel_id=1, replica_groups=mesh['ctx'=16,'exp'=32] {'ctx'}, dimensions={0} | all-to-all | bytes 524288 | tf_op jit(solution)/shard_map/all_to_all | solution.py:321
  191.4 0.6 reduce_sum.42
  (7 shorter events, 0.1 us)
Async XLA Ops:
  0.6 45.0 %copy-start = (bf16[256,128]{1,0:T(8,128)(2,1)S(1)}, bf16[256,128]{1,0:T(8,128)(2,1)}, u32[]{:S(2)}) copy-start(bf16[256,128]{1,0:T(8,128)(2,1)} %proj_ref.3) | copy-start | bytes 196612
  0.7 45.0 %copy-start.2 = (bf16[64,128]{1,0:T(8,128)(2,1)S(1)}, bf16[64,128]{1,0:T(8,128)(2,1)}, u32[]{:S(2)}) copy-start(bf16[64,128]{1,0:T(8,128)(2,1)} %query_ref.1) | copy-start | bytes 49156
  0.7 45.0 %copy-start.3 = (f32[64,2]{0,1:T(2,128)S(1)}, f32[64,2]{0,1:T(2,128)}, u32[]{:S(2)}) copy-start(f32[64,2]{0,1:T(2,128)} %param.18) | copy-start | bytes 1540
  0.7 45.0 %copy-start.4 = (f32[128]{0:T(128)S(1)}, f32[128]{0:T(128)}, u32[]{:S(2)}) copy-start(f32[128]{0:T(128)} %param.16) | copy-start | bytes 1540
  4.3 49.8 %copy-start.5 = (s32[1024,2]{0,1:T(2,128)S(1)}, s32[1024,2]{0,1:T(2,128)}, u32[]{:S(2)}) copy-start(s32[1024,2]{0,1:T(2,128)} %param.17) | copy-start | bytes 24580
  4.3 85.1 %collective-permute-start = (bf16[12288,128]{1,0:T(8,128)(2,1)}, bf16[12288,128]{1,0:T(8,128)(2,1)}, u32[]{:S(2)}, u32[]{:S(2)}) collective-permute-start(bf16[12288,128]{1,0:T(8,128)(2,1)} %get-tuple-element.17.near_ref), channel_id=1, source_target_pairs={{0,2},{1,3},{2,0},{3,1},{4,6},{5,7},{6,4},{7,5},{8,10},{9,11},{10,... | collective-permute-start | bytes 9437192 | tf_op jit(solution)/shard_map/ppermute | solution.py:281
  7.7 80.7 %copy-start.1 = (bf16[64,128]{1,0:T(8,128)(2,1)S(1)}, bf16[64,128]{1,0:T(8,128)(2,1)}, u32[]{:S(2)}) copy-start(bf16[64,128]{1,0:T(8,128)(2,1)} %residual_ref.1) | copy-start | bytes 49156
  47.0 41.4 %all-to-all-start = ((bf16[32,80,128]{2,1,0:T(8,128)(2,1)}), bf16[32,80,128]{2,1,0:T(8,128)(2,1)S(1)}, u32[]{:S(2)}, u32[]{:S(2)}) async-start(bf16[32,80,128]{2,1,0:T(8,128)(2,1)} %get-tuple-element.12), calls=%async_computation | async-start | bytes 1310720 | tf_op jit(solution)/shard_map/all_to_all | solution.py:292
  89.5 51.2 %collective-permute-start.1 = (bf16[12288,128]{1,0:T(8,128)(2,1)}, bf16[12288,128]{1,0:T(8,128)(2,1)}, u32[]{:S(2)}, u32[]{:S(2)}) collective-permute-start(bf16[12288,128]{1,0:T(8,128)(2,1)} %get-tuple-element.18.refs_0_), channel_id=1, source_target_pairs={{0,1},{1,0},{2,3},{3,2},{4,5},{5,4},{6,7},{7,6},{8,9},{9,8},{10,11... | collective-permute-start | bytes 9437192 | tf_op jit(solution)/shard_map/ppermute | solution.py:309
  91.4 49.2 %collective-permute-start.2 = (bf16[12288,128]{1,0:T(8,128)(2,1)}, bf16[12288,128]{1,0:T(8,128)(2,1)}, u32[]{:S(2)}, u32[]{:S(2)}) collective-permute-start(bf16[12288,128]{1,0:T(8,128)(2,1)} %get-tuple-element.19.refs_2_), channel_id=1, source_target_pairs={{0,1},{1,0},{2,3},{3,2},{4,5},{5,4},{6,7},{7,6},{8,9},{9,8},{10,11... | collective-permute-start | bytes 9437192 | tf_op jit(solution)/shard_map/ppermute | solution.py:310
  148.0 15.7 %all-to-all-start.2 = ((bf16[32,64,128]{2,1,0:T(8,128)(2,1)}), bf16[32,64,128]{2,1,0:T(8,128)(2,1)S(1)}, u32[]{:S(2)}, u32[]{:S(2)}) async-start(bf16[32,64,128]{2,1,0:T(8,128)(2,1)} %shard_map.126), calls=%async_computation.2 | async-start | bytes 1048576 | tf_op jit(solution)/shard_map/all_to_all | solution.py:320
